TPU v7x, 128 devices: a whole 4x4x4 slice. The times are simulated.
128 devices in a mesh: tm: 4 (over y_lo, core), space: 32 (over x, z, y_hi).
Axes of the slice: x: 4, y: 4 (y_hi: 2, y_lo: 2; y = y_hi * 2 + y_lo), z: 4, core: 2. Of those that a mesh axis runs over, the one named last changes fastest.
Arguments:
- hidden_state: bfloat16 [16, 32, 2, 8, 512], P('tm', 'space'), may hold values from -20 to 20
- norm1_gain: float32 [512], replicated, may hold values from 0.25 to 1.75
- norm1_bias: float32 [512], replicated, may hold values from -3 to 3
- qkv_weight: bfloat16 [512, 1536], replicated, may hold values from -8 to 8
- out_weight: bfloat16 [512, 512], replicated, may hold values from -0.25 to 0.25
- out_bias: float32 [512], replicated, may hold values from -3 to 3
- conv1_weight: bfloat16 [3, 3, 3, 512, 512], replicated, may hold values from -0.0546875 to 0.0546875
- conv1_bias: float32 [512], replicated, may hold values from -3 to 3
- norm2_gain: float32 [512], replicated, may hold values from 0.25 to 1.75
- norm2_bias: float32 [512], replicated, may hold values from -3 to 3
- conv2_weight: bfloat16 [3, 3, 3, 512, 256], replicated, may hold values from -0.0546875 to 0.0546875
- conv2_bias: float32 [256], replicated, may hold values from -3 to 3
Outputs:
- decoded: bfloat16 [16, 32, 8, 32, 256], P('tm', 'space')
All inputs are finite; a program needn't handle non-finite values.
Results may differ from a plain program's by a relative error of at most 0.017.
Values may be sent and summed in bfloat16 or wider, within the bound.
A program may use at most 128 MiB of HBM per device.

v0:
```python
import jax
import jax.numpy as jnp
from jax import lax
from jax.sharding import PartitionSpec as P

GROUPS = 32
GRID_W = 4


def shifted(value, axis, steps):
    count = lax.axis_size(axis)
    leading, last = (max(0, -steps), min(count, count - steps))
    return lax.ppermute(value, axis, [(source, source + steps) for source in range(leading, last)])


def frame_norm(field, gain, bias):
    frames, height, width, chans = field.shape
    grouped = field.astype(jnp.float32).reshape(frames, height, width, GROUPS, chans // GROUPS)
    first_sum = jnp.sum(grouped, axis=(1, 2, 4))
    second_sum = jnp.sum(grouped * grouped, axis=(1, 2, 4))
    first_sum, second_sum = lax.psum((first_sum, second_sum), "space")
    count = height * width * lax.axis_size("space") * (chans // GROUPS)
    mean_val = first_sum / count
    var_val = second_sum / count - mean_val * mean_val
    scaled = (grouped - mean_val[:, None, None, :, None]) * lax.rsqrt(var_val + 1e-06)[
        :, None, None, :, None
    ]
    return scaled.reshape(frames, height, width, chans) * gain + bias


def project_heads(features, qkv_weight):
    frames, cells, chans = features.shape
    projected = jnp.dot(features.reshape(-1, chans), qkv_weight, preferred_element_type=jnp.float32)
    queries = projected[:, :chans].astype(jnp.bfloat16).reshape(frames, cells, chans)
    keys = projected[:, chans : 2 * chans].astype(jnp.bfloat16).reshape(frames, cells, chans)
    values = projected[:, 2 * chans :].astype(jnp.bfloat16).reshape(frames, cells, chans)
    return (queries, keys, values)


def gathered_attention(features, qkv_weight):
    frames, cells, chans = features.shape
    queries, keys, values = project_heads(features, qkv_weight)
    query_pos = lax.axis_index("tm") * frames + jnp.arange(frames, dtype=jnp.int32)
    running_max = jnp.full((frames, cells), -1e30, jnp.float32)
    key_piece = lax.all_gather(keys, "tm", axis=0, tiled=True)
    value_piece = lax.all_gather(values, "tm", axis=0, tiled=True)
    key_pos = jnp.arange(key_piece.shape[0], dtype=jnp.int32)
    scores = jnp.einsum(
        "fpc,gpc->fpg", queries, key_piece, preferred_element_type=jnp.float32
    ) * chans ** (-0.5)
    allowed = key_pos[None, None, :] <= query_pos[:, None, None]
    new_max = jnp.maximum(running_max, jnp.max(jnp.where(allowed, scores, -1e30), axis=-1))
    weights = jnp.where(allowed, jnp.exp(scores - new_max[..., None]), 0.0)
    new_total = jnp.sum(weights, axis=-1)
    update = jnp.einsum(
        "fpg,gpc->fpc",
        weights.astype(jnp.bfloat16),
        value_piece,
        preferred_element_type=jnp.float32,
    )
    return (update / new_total[..., None]).astype(jnp.bfloat16)


def extend_block(tile_block):
    received = shifted(tile_block[-2:], "tm", 1)
    starting = lax.axis_index("tm") == 0
    leading = jnp.where(
        starting, jnp.concatenate([tile_block[:1], tile_block[:1]], axis=0), received
    )
    timed = jnp.concatenate([leading, tile_block], axis=0)
    tile_column = lax.axis_index("space") % GRID_W
    from_left = shifted(timed[:, :, -1:], "space", 1)
    from_left = jnp.where(tile_column == 0, jnp.zeros_like(from_left), from_left)
    from_right = shifted(timed[:, :, :1], "space", -1)
    from_right = jnp.where(tile_column == GRID_W - 1, jnp.zeros_like(from_right), from_right)
    widened = jnp.concatenate([from_left, timed, from_right], axis=2)
    from_above = shifted(widened[:, -1:], "space", GRID_W)
    from_below = shifted(widened[:, :1], "space", -GRID_W)
    return jnp.concatenate([from_above, widened, from_below], axis=1)


def upsample_conv(tile_block, weight, bias):
    frames, height, width, chans = tile_block.shape
    outs = weight.shape[-1]
    extended = extend_block(tile_block)
    upsampled = jnp.repeat(jnp.repeat(extended, 2, axis=1), 2, axis=2)[:, 1:-1, 1:-1]
    total = jnp.zeros((frames * 2 * height * 2 * width, outs), jnp.float32)
    for time_offset in range(3):
        for row_offset in range(3):
            pieces = [
                upsampled[
                    time_offset : time_offset + frames,
                    row_offset : row_offset + 2 * height,
                    column_offset : column_offset + 2 * width,
                ]
                for column_offset in range(3)
            ]
            slab = jnp.concatenate(pieces, axis=-1).reshape(-1, 3 * chans)
            total = total + jnp.dot(
                slab,
                weight[time_offset, row_offset].reshape(3 * chans, outs),
                preferred_element_type=jnp.float32,
            )
    return total.reshape(frames, 2 * height, 2 * width, outs) + bias


def per_device(
    hidden_state,
    norm1_gain,
    norm1_bias,
    qkv_weight,
    out_weight,
    out_bias,
    conv1_weight,
    conv1_bias,
    norm2_gain,
    norm2_bias,
    conv2_weight,
    conv2_bias,
):
    tile_block = hidden_state[:, 0]
    frames, height, width, chans = tile_block.shape
    normed = frame_norm(tile_block, norm1_gain, norm1_bias).astype(jnp.bfloat16)
    features = normed.reshape(frames, height * width, chans)
    attended = gathered_attention(features, qkv_weight)
    output_proj = (
        jnp.dot(attended.reshape(-1, chans), out_weight, preferred_element_type=jnp.float32)
        + out_bias
    )
    mixed = (tile_block.astype(jnp.float32) + output_proj.reshape(tile_block.shape)).astype(
        jnp.bfloat16
    )
    first_section = upsample_conv(mixed, conv1_weight, conv1_bias).astype(jnp.bfloat16)
    activated = jax.nn.silu(frame_norm(first_section, norm2_gain, norm2_bias)).astype(jnp.bfloat16)
    decoded = upsample_conv(activated, conv2_weight, conv2_bias).astype(jnp.bfloat16)
    return decoded[:, None]


def solution(mesh):
    return jax.shard_map(
        per_device,
        mesh=mesh,
        in_specs=(
            P("tm", "space", None, None, None),
            P(),
            P(),
            P(),
            P(),
            P(),
            P(),
            P(),
            P(),
            P(),
            P(),
            P(),
        ),
        out_specs=P("tm", "space", None, None, None),
        check_vma=False,
    )
```

profile of v0, /device:TPU:1, one launch (start us, length us, event | category | flops | bytes accessed | tf_op | source)
XLA Modules:
  0.0 331.1 jit_solution(8797310520580933753)
XLA Ops:
  0.1 1.0 convert_reduce_fusion.1
  1.5 84.6 %all-reduce.1 = (f32[4,32]{1,0:T(4,128)S(1)}, f32[4,32]{1,0:T(4,128)S(1)}) all-reduce(f32[4,32]{1,0:T(4,128)S(1)} %reduce_sum.64, f32[4,32]{1,0:T(4,128)S(1)} %reduce_sum.61), channel_id=1, replica_groups=mesh['tm'=4,'space'=32] {'space'}, use_global_device_ids=true, to_apply=%region_5.6 | all-reduce | flops 256 | bytes 2048 | tf_op jit(solution)/shard_map/psum | solution.py:21
  86.5 0.9 fusion.8
  87.8 20.3 %all_gather.7 = bf16[16,16,512]{2,1,0:T(8,128)(2,1)S(1)} all-gather(bf16[4,16,512]{2,1,0:T(8,128)(2,1)S(1)} %bitcast.158), channel_id=1, replica_groups=mesh['tm'=4,'space'=32] {'tm'}, dimensions={0}, use_global_device_ids=true | all-gather | bytes 327680 | tf_op jit(solution)/shard_map/all_gather | solution.py:45
  108.5 5.9 %all_gather.6 = bf16[16,16,512]{2,1,0:T(8,128)(2,1)S(1)} all-gather(bf16[4,16,512]{2,1,0:T(8,128)(2,1)S(1)} %bitcast.157), channel_id=1, replica_groups=mesh['tm'=4,'space'=32] {'tm'}, dimensions={0}, use_global_device_ids=true | all-gather | bytes 327680 | tf_op jit(solution)/shard_map/all_gather | solution.py:46
  115.1 2.3 collective-permute-start
  117.4 1.0 collective-permute-done
  118.5 1.3 collective-permute-start.1
  119.8 1.3 collective-permute-start.2
  121.1 4.7 %collective-permute-done.2 = bf16[6,2,1,512]{3,2,1,0:T(2,128)(2,1)S(1)} collective-permute-done((bf16[6,2,1,512]{3,2,1,0:T(2,128)(2,1)S(1)}, bf16[6,2,1,512]{3,2,1,0:T(2,128)(2,1)S(1)}, u32[]{:S(2)}, u32[]{:S(2)}) %collective-permute-start.2) | collective-permute-done | bytes 12320 | tf_op jit(solution)/shard_map/ppermute | solution.py:13
  126.0 1.9 collective-permute-start.3
  127.9 1.6 collective-permute-start.4
  129.5 9.0 %fusion.18 = (bf16[1,1,3,512,512]{4,3,2,1,0:T(8,128)(2,1)S(1)}, bf16[1,1,3,512,512]{4,3,2,1,0:T(8,128)(2,1)}, bf16[1,1,3,512,512]{4,3,2,1,0:T(8,128)(2,1)}, bf16...) fusion(bf16[3,3,3,512,512]{4,3,2,1,0:T(8,128)(2,1)} %param.18), kind=kLoop, calls=%fused_computation.92 | loop fusion | bytes 28311552 | tf_op jit(solution)/shard_map/slice | solution.py:101
  138.7 1.1 pad_maximum_fusion.19
  139.9 1.1 broadcast_in_dim.53
  141.1 2.0 reshape.173
  143.1 1.1 broadcast_in_dim.54
  144.9 3.1 fusion.22
  159.3 2.8 reshape.185
  162.1 3.2 convert_reduce_fusion
  165.3 79.3 %all-reduce = (f32[4,32]{1,0:T(4,128)S(1)}, f32[4,32]{1,0:T(4,128)S(1)}) all-reduce(f32[4,32]{1,0:T(4,128)S(1)} %get-tuple-element.6, f32[4,32]{1,0:T(4,128)S(1)} %get-tuple-element.5), channel_id=1, replica_groups=mesh['tm'=4,'space'=32] {'space'}, use_global_device_ids=true, to_apply=%region_11.12 | all-reduce | flops 256 | bytes 2048 | tf_op jit(solution)/shard_map/psum | solution.py:21
  245.2 19.6 %collective-permute-start.5 = (bf16[2,4,16,512]{3,2,1,0:T(8,128)(2,1)S(1)}, bf16[2,4,16,512]{3,2,1,0:T(8,128)(2,1)S(1)}, u32[]{:S(2)}, u32[]{:S(2)}) collective-permute-start(bf16[2,4,16,512]{3,2,1,0:T(8,128)(2,1)S(1)} %slice.444), channel_id=1, source_target_pairs={{0,32},{32,64},{64,96},{1,33},{33,65},{65,97},{2,34},{34,66},{66,9... | collective-permute-start | bytes 393224 | tf_op jit(solution)/shard_map/ppermute | solution.py:13
  264.8 2.2 collective-permute-done.5
  267.1 2.0 collective-permute-start.6
  269.1 1.3 collective-permute-start.7
  270.5 5.0 %collective-permute-done.7 = bf16[6,4,1,512]{3,2,1,0:T(2,128)(2,1)S(1)} collective-permute-done((bf16[6,4,1,512]{3,2,1,0:T(2,128)(2,1)S(1)}, bf16[6,4,1,512]{3,2,1,0:T(2,128)(2,1)S(1)}, u32[]{:S(2)}, u32[]{:S(2)}) %collective-permute-start.7) | collective-permute-done | bytes 24608 | tf_op jit(solution)/shard_map/ppermute | solution.py:13
  275.7 1.3 collective-permute-start.8
  277.0 1.5 collective-permute-start.9
  278.5 6.1 %fusion.19 = (bf16[1,1,3,512,256]{4,3,2,1,0:T(8,128)(2,1)}, bf16[1,1,3,512,256]{4,3,2,1,0:T(8,128)(2,1)}, bf16[1,1,3,512,256]{4,3,2,1,0:T(8,128)(2,1)}, bf16[1,1...) fusion(bf16[3,3,3,512,256]{4,3,2,1,0:T(8,128)(2,1)} %param.22), kind=kLoop, calls=%fused_computation.93 | loop fusion | bytes 14155776 | tf_op jit(solution)/shard_map/slice | solution.py:101
  285.1 3.1 broadcast_in_dim.56
  288.2 5.6 %reshape.187 = bf16[6,12,36,512]{3,2,1,0:T(8,128)(2,1)S(1)} reshape(bf16[6,12,18,2,512]{4,3,2,1,0:T(2,128)(2,1)} %broadcast_in_dim.56) | data formatting | bytes 5308416 | tf_op jit(solution)/shard_map/reshape | solution.py:86
  293.8 4.2 %fusion.21 = (bf16[4,8,32,512]{3,2,1,0:T(8,128)(2,1)}, bf16[4,8,32,512]{3,2,1,0:T(8,128)(2,1)}, bf16[4,8,32,512]{3,2,1,0:T(8,128)(2,1)}, bf16[4,8,32,512]{3,2,1,...) fusion(bf16[6,12,36,512]{3,2,1,0:T(8,128)(2,1)S(1)} %reshape.187), kind=kLoop, calls=%fused_computation.95 | loop fusion | bytes 16777216 | tf_op jit(solution)/shard_map/slice | solution.py:91
  298.0 8.5 %fusion.20 = (bf16[4,8,32,512]{3,2,1,0:T(8,128)(2,1)}, bf16[4,8,32,512]{3,2,1,0:T(8,128)(2,1)}, bf16[4,8,32,512]{3,2,1,0:T(8,128)(2,1)}, bf16[4,8,32,512]{3,2,1,...) fusion(bf16[6,12,36,512]{3,2,1,0:T(8,128)(2,1)S(1)} %reshape.187), kind=kLoop, calls=%fused_computation.94 | loop fusion | bytes 39845888 | tf_op jit(solution)/shard_map/slice | solution.py:91
  306.6 2.1 pad_maximum_fusion
  308.7 1.0 fusion.27
  310.8 0.8 copy-done.33
  311.7 1.0 convolution_add_fusion.7
  313.8 0.9 copy-done.17
  316.5 1.0 convolution_add_fusion.6
  318.7 0.9 copy-done.11
  320.5 0.9 copy-done.9
  323.5 1.0 convolution_add_fusion.5
  324.6 1.0 convolution_add_fusion.4
  325.7 1.0 convolution_add_fusion.3
  326.9 1.0 convolution_add_fusion.2
  328.0 1.0 convolution_add_fusion.1
  329.2 1.0 convolution_add_fusion
  330.1 0.9 add_convert_fusion.1
  (163 shorter events, 25.0 us)
Async XLA Ops:
  0.0 87.4 %copy-start = (bf16[512,1536]{1,0:T(8,128)(2,1)S(1)}, bf16[512,1536]{1,0:T(8,128)(2,1)}, u32[]{:S(2)}) copy-start(bf16[512,1536]{1,0:T(8,128)(2,1)} %param.15) | copy-start | bytes 4718596
  0.0 114.9 %copy-start.38 = (f32[512]{0:T(512)S(1)}, f32[512]{0:T(512)}, u32[]{:S(2)}) copy-start(f32[512]{0:T(512)} %param.17) | copy-start | bytes 6148
  0.0 114.9 %copy-start.36 = (bf16[512,512]{1,0:T(8,128)(2,1)S(1)}, bf16[512,512]{1,0:T(8,128)(2,1)}, u32[]{:S(2)}) copy-start(bf16[512,512]{1,0:T(8,128)(2,1)} %param.16) | copy-start | bytes 1572868
  1.5 113.6 %copy-start.35 = (bf16[4,1,2,8,512]{4,3,2,1,0:T(8,128)(2,1)S(1)}, bf16[4,1,2,8,512]{4,3,2,1,0:T(8,128)(2,1)}, u32[]{:S(2)}) copy-start(bf16[4,1,2,8,512]{4,3,2,1,0:T(8,128)(2,1)} %param.12) | copy-start | bytes 196612
  115.1 3.3 collective-permute-start
  118.5 2.6 collective-permute-start.1
  119.8 6.1 %collective-permute-start.2 = (bf16[6,2,1,512]{3,2,1,0:T(2,128)(2,1)S(1)}, bf16[6,2,1,512]{3,2,1,0:T(2,128)(2,1)S(1)}, u32[]{:S(2)}, u32[]{:S(2)}) collective-permute-start(bf16[6,2,1,512]{3,2,1,0:T(2,128)(2,1)S(1)} %get-tuple-element.95), channel_id=1, source_target_pairs={{1,0},{2,1},{3,2},{4,3},{5,4},{6,5},{7,6},{8,7},{9,8},{10,9},{11,1... | collective-permute-start | bytes 36872 | tf_op jit(solution)/shard_map/ppermute | solution.py:13
  126.0 12.7 %collective-permute-start.3 = (bf16[6,1,10,512]{3,2,1,0:T(8,128)(2,1)S(1)}, bf16[6,1,10,512]{3,2,1,0:T(8,128)(2,1)}, u32[]{:S(2)}, u32[]{:S(2)}) collective-permute-start(bf16[6,1,10,512]{3,2,1,0:T(8,128)(2,1)S(1)} %get-tuple-element.89), channel_id=1, source_target_pairs={{0,4},{1,5},{2,6},{3,7},{4,8},{5,9},{6,10},{7,11},{8,12},{9,13},{1... | collective-permute-start | bytes 184328 | tf_op jit(solution)/shard_map/ppermute | solution.py:13
  127.9 10.6 %copy-start.37 = (f32[512]{0:T(512)S(1)}, f32[512]{0:T(512)}, u32[]{:S(2)}) copy-start(f32[512]{0:T(512)} %param.19) | copy-start | bytes 6148
  127.9 10.7 %collective-permute-start.4 = (bf16[6,1,10,512]{3,2,1,0:T(8,128)(2,1)S(1)}, bf16[6,1,10,512]{3,2,1,0:T(8,128)(2,1)}, u32[]{:S(2)}, u32[]{:S(2)}) collective-permute-start(bf16[6,1,10,512]{3,2,1,0:T(8,128)(2,1)S(1)} %get-tuple-element.90), channel_id=1, source_target_pairs={{4,0},{5,1},{6,2},{7,3},{8,4},{9,5},{10,6},{11,7},{12,8},{13,9},{1... | collective-permute-start | bytes 184328 | tf_op jit(solution)/shard_map/ppermute | solution.py:13
  151.6 1.4 copy-start.8
  152.3 1.5 copy-start.7
  153.0 1.5 copy-start.6
  153.9 1.5 copy-start.5
  154.5 1.5 copy-start.4
  155.4 1.5 copy-start.3
  156.1 1.5 copy-start.2
  162.1 82.9 %copy-start.39 = (f32[512]{0:T(512)S(1)}, f32[512]{0:T(512)}, u32[]{:S(2)}) copy-start(f32[512]{0:T(512)} %param.21) | copy-start | bytes 6148
  162.1 82.9 %copy-start.40 = (f32[512]{0:T(512)S(1)}, f32[512]{0:T(512)}, u32[]{:S(2)}) copy-start(f32[512]{0:T(512)} %param.20) | copy-start | bytes 6148
  245.2 21.8 %collective-permute-start.5 = (bf16[2,4,16,512]{3,2,1,0:T(8,128)(2,1)S(1)}, bf16[2,4,16,512]{3,2,1,0:T(8,128)(2,1)S(1)}, u32[]{:S(2)}, u32[]{:S(2)}) collective-permute-start(bf16[2,4,16,512]{3,2,1,0:T(8,128)(2,1)S(1)} %slice.444), channel_id=1, source_target_pairs={{0,32},{32,64},{64,96},{1,33},{33,65},{65,97},{2,34},{34,66},{66,9... | collective-permute-start | bytes 393224 | tf_op jit(solution)/shard_map/ppermute | solution.py:13
  267.1 3.3 %collective-permute-start.6 = (bf16[6,4,1,512]{3,2,1,0:T(2,128)(2,1)S(1)}, bf16[6,4,1,512]{3,2,1,0:T(2,128)(2,1)S(1)}, u32[]{:S(2)}, u32[]{:S(2)}) collective-permute-start(bf16[6,4,1,512]{3,2,1,0:T(2,128)(2,1)S(1)} %get-tuple-element.87), channel_id=1, source_target_pairs={{0,1},{1,2},{2,3},{3,4},{4,5},{5,6},{6,7},{7,8},{8,9},{9,10},{10,1... | collective-permute-start | bytes 73736 | tf_op jit(solution)/shard_map/ppermute | solution.py:13
  269.1 6.3 %collective-permute-start.7 = (bf16[6,4,1,512]{3,2,1,0:T(2,128)(2,1)S(1)}, bf16[6,4,1,512]{3,2,1,0:T(2,128)(2,1)S(1)}, u32[]{:S(2)}, u32[]{:S(2)}) collective-permute-start(bf16[6,4,1,512]{3,2,1,0:T(2,128)(2,1)S(1)} %get-tuple-element.88), channel_id=1, source_target_pairs={{1,0},{2,1},{3,2},{4,3},{5,4},{6,5},{7,6},{8,7},{9,8},{10,9},{11,1... | collective-permute-start | bytes 73736 | tf_op jit(solution)/shard_map/ppermute | solution.py:13
  275.7 8.9 %collective-permute-start.8 = (bf16[6,1,18,512]{3,2,1,0:T(8,128)(2,1)S(1)}, bf16[6,1,18,512]{3,2,1,0:T(8,128)(2,1)S(1)}, u32[]{:S(2)}, u32[]{:S(2)}) collective-permute-start(bf16[6,1,18,512]{3,2,1,0:T(8,128)(2,1)S(1)} %get-tuple-element.85), channel_id=1, source_target_pairs={{0,4},{1,5},{2,6},{3,7},{4,8},{5,9},{6,10},{7,11},{8,12},{9,13},{1... | collective-permute-start | bytes 331784 | tf_op jit(solution)/shard_map/ppermute | solution.py:13
  277.0 7.6 %collective-permute-start.9 = (bf16[6,1,18,512]{3,2,1,0:T(8,128)(2,1)S(1)}, bf16[6,1,18,512]{3,2,1,0:T(8,128)(2,1)S(1)}, u32[]{:S(2)}, u32[]{:S(2)}) collective-permute-start(bf16[6,1,18,512]{3,2,1,0:T(8,128)(2,1)S(1)} %get-tuple-element.86), channel_id=1, source_target_pairs={{4,0},{5,1},{6,2},{7,3},{8,4},{9,5},{10,6},{11,7},{12,8},{13,9},{1... | collective-permute-start | bytes 331784 | tf_op jit(solution)/shard_map/ppermute | solution.py:13
  306.6 2.1 copy-start.34
  308.7 1.2 copy-start.23
  308.7 1.5 copy-start.24
  308.7 1.8 copy-start.25
  310.5 1.1 copy-start.33
  311.7 1.2 copy-start.20
  311.7 1.5 copy-start.21
  311.7 1.9 copy-start.22
  313.5 1.2 copy-start.17
  313.5 1.5 copy-start.18
  313.5 1.9 copy-start.19
  315.4 1.1 copy-start.32
  316.5 1.2 copy-start.14
  316.5 1.5 copy-start.15
  316.5 1.9 copy-start.16
  318.4 1.2 copy-start.11
  318.4 1.5 copy-start.12
  318.4 1.9 copy-start.13
  320.2 1.2 copy-start.9
  320.2 1.5 copy-start.10
  322.3 1.1 copy-start.31
  324.6 1.1 copy-start.29
  325.7 1.1 copy-start.28
  329.0 2.1 copy-start.1
  (4 other events, 4.4 us)
where the time goes:
time: 334 us; the launch traced here: 331 us
  blocking collectives  190 us (57%)
  local copies, waits for them, and re-layouts  61.4 us (18%)
  starting transfers between devices  34.1 us (10%)
  other arithmetic  16.6 us (5%)
  matrix products  15.2 us (5%)
  waiting for transfers between devices  12.9 us (4%)
    psum x2, blocking collectives, frame_norm(): first_sum, second_sum = lax.psum((first_sum, second_sum), 'space')  164 us
    ppermute x10, starting transfers between devices, shifted(): lax.ppermute(value, axis, [(source, source + steps) for source in range(l...  34.1 us
    all_gather x1, blocking collectives, gathered_attention(): key_piece = lax.all_gather(keys, 'tm', axis=0, tiled=True)  20.3 us
    slice x4, local copies, waits for them, and re-layouts, upsample_conv(): upsampled[time_offset:time_offset + frames, row_offset:row_offset + 2 * h...  16.5 us
    slice x2, local copies, waits for them, and re-layouts, upsample_conv(): weight[time_offset, row_offset].reshape(3 * chans, outs)  15.1 us
    dot_general x18, matrix products, upsample_conv(): jnp.dot(slab, weight[time_offset, row_offset].reshape(3 * chans, outs), p...  13.9 us
    ppermute x10, waiting for transfers between devices, shifted(): lax.ppermute(value, axis, [(source, source + steps) for source in range(l...  12.9 us
    unnamed x84, local copies, waits for them, and re-layouts  11.3 us
  transfers between devices with their start and end apart: 10, of which 4 were waited for; matrix products, arithmetic and copies ran while one was open for 5% of the time, Pallas kernels for 0%

commit v1 on v0

v1 whole, which is shorter than its diff:
```python
import jax
import jax.numpy as jnp
from jax import lax
from jax.experimental import pallas as pl
from jax.experimental.pallas import tpu as pltpu
from jax.sharding import PartitionSpec as P

F32, BF16 = jnp.float32, jnp.bfloat16
MESH = pl.DeviceIdType.MESH
C, C2, LANES = 512, 256, 128
CHUNKS = C // LANES
GRID_COLS, GRID_ROWS, TILES, SHARDS = 4, 8, 32, 4
FRAMES = 4
CELLS = 40
FAR = 21
EPS = 1e-6
RING = ((-1, 0), (1, 0), (0, -1), (0, 1), (-1, -1), (-1, 1), (1, -1), (1, 1))
RING_ROWS = (32, 32, 16, 16, 16, 16, 16, 16)
RING_AT = (64, 96, 128, 144, 160, 176, 192, 208)
BLOCK_ROWS = 224


def iota(shape, axis):
    return lax.broadcasted_iota(jnp.int32, shape, axis)


def lane_roll(value, shift):
    return pltpu.roll(value, shift % LANES, axis=value.ndim - 1)


def sub_roll(value, shift):
    return pltpu.roll(value, shift % 8, axis=value.ndim - 2)


def pack_sums(total, first_row):
    lane = iota((8, LANES), 1)
    row = iota((8, LANES), 0)
    merged = jnp.zeros((8, LANES), F32)
    for k in range(CHUNKS):
        part = total[:, k * LANES : (k + 1) * LANES]
        for step in (1, 2, 4, 8):
            part = part + lane_roll(part, -step)
        part = jnp.where((lane & 15) == 0, part, 0.0)
        merged = merged + (lane_roll(part, k) if k else part)
    placed = jnp.zeros((8, LANES), F32)
    for f in range(FRAMES):
        placed = placed + jnp.where(row == first_row + f, lane_roll(merged, 4 * f) if f else merged, 0.0)
    return jnp.sum(placed, axis=0, keepdims=True)


def group_stats(block, count):
    total = jnp.sum(block.reshape(8, 8, LANES), axis=0)
    total = total + sub_roll(total, 2)
    total = total + sub_roll(total, 4)
    mean = total[0:1] * (1.0 / count)
    square = total[1:2] * (1.0 / count)
    scale = lax.rsqrt(square - mean * mean + EPS)
    return jnp.broadcast_to(mean, (8, LANES)), jnp.broadcast_to(scale, (8, LANES))


def by_frame(first, second, second_rows, frames):
    row = iota((8, LANES), 0)
    out = jnp.zeros((8, LANES), F32)
    for f in range(FRAMES):
        moved = (lane_roll(first, -4 * f), lane_roll(second, -4 * f)) if f else (first, second)
        for r in range(8):
            if frames[r] == f:
                out = jnp.where(row == r, moved[1] if second_rows[r] else moved[0], out)
    return out


def spread(rows):
    lane = iota((8, LANES), 1)
    parts = []
    for k in range(CHUNKS):
        part = jnp.where((lane & 15) == 0, lane_roll(rows, -k) if k else rows, 0.0)
        for step in (1, 2, 4, 8):
            part = part + lane_roll(part, step)
        parts.append(part)
    return jnp.concatenate(parts, axis=1)


def kernel(
    hid_hbm, gain1_hbm, bias1_hbm, wqkv_hbm, wout_hbm, bout_hbm, w1_hbm, b1_hbm, gain2_hbm, bias2_hbm, w2_hbm, b2_hbm,
    out_ref,
    hid, gain1, bias1, wqkv, wout, bout, w1, b1, gain2, bias2, w2, b2,
    own, side, hbuf, sums, got1, got2, xhi, normed, queries, keys, values, attended, mixcat, t1, fs, actcat, t2,
    small_sem, w1_sem, w2_sem, hid_send, hid_recv, sum_send, sum_recv,
):
    tm = lax.axis_index("tm")
    sp = lax.axis_index("space")
    tile_row, tile_col = sp >> 2, sp & 3

    smalls = [
        pltpu.make_async_copy(a, b, small_sem.at[i])
        for i, (a, b) in enumerate(
            (
                (hid_hbm, hid), (wqkv_hbm, wqkv), (wout_hbm, wout), (gain1_hbm, gain1), (bias1_hbm, bias1),
                (bout_hbm, bout), (b1_hbm, b1), (gain2_hbm, gain2), (bias2_hbm, bias2), (b2_hbm, b2),
            )
        )
    ]
    for copy in smalls:
        copy.start()

    barrier = pltpu.get_barrier_semaphore()
    for kt in range(SHARDS):
        def greet(i, carry, kt=kt):
            ks = i ^ FAR

            def signal():
                pl.semaphore_signal(barrier, inc=1, device_id=(tm ^ kt, sp ^ ks), device_id_type=MESH)

            if kt:
                signal()
            else:
                pl.when(ks != 0)(signal)
            return carry

        lax.fori_loop(0, TILES, greet, 0)

    def tap_copies(i):
        a, be = i // 9, lax.rem(i, 9)
        rows = pl.ds(pl.multiple_of(a * C, C), C)
        return (
            pltpu.make_async_copy(w1_hbm.at[i], w1.at[be, rows], w1_sem.at[i]),
            pltpu.make_async_copy(w2_hbm.at[i], w2.at[be, rows], w2_sem.at[i]),
        )

    def start_first(i, carry):
        tap_copies(i)[0].start()
        return carry

    def start_second(i, carry):
        tap_copies(i)[1].start()
        return carry

    lax.fori_loop(0, 27, start_first, 0)
    lax.fori_loop(0, 27, start_second, 0)

    for dt in range(1, SHARDS):
        @pl.when(tm < dt)
        def _():
            hbuf[3 - dt] = jnp.zeros((BLOCK_ROWS, C), BF16)

    for copy in smalls:
        copy.wait()
    order_out, order_in = iota((64, 64), 0), iota((64, 64), 1)
    wanted = (order_out & 3) * 16 + (order_out >> 2)
    permute = jnp.where(order_in == wanted, 1.0, 0.0).astype(BF16)
    plain = hid[...].astype(F32).reshape(64, C).astype(BF16)
    mine = jnp.dot(permute, plain, preferred_element_type=F32)
    mine16 = mine.astype(BF16)
    own[...] = mine16
    hbuf[3, 0:64] = mine16
    side[0] = jnp.concatenate([mine[0:8], mine[32:40]], axis=0).astype(BF16)
    side[1] = jnp.concatenate([mine[24:32], mine[56:64]], axis=0).astype(BF16)
    pairs = mine.reshape(8, 8, C)
    first = jnp.sum(pairs, axis=0)
    second = jnp.sum(pairs * pairs, axis=0)
    first = first + sub_roll(first, 4)
    second = second + sub_roll(second, 4)
    packed = jnp.concatenate([pack_sums(first, 0), pack_sums(second, 0)], axis=0)
    sums[0] = packed
    got1[0:2] = packed

    pl.semaphore_wait(barrier, SHARDS * TILES - 1)

    def send_sums(which, target, slot, buf):
        pltpu.make_async_remote_copy(
            src_ref=sums.at[which], dst_ref=buf.at[pl.ds(pl.multiple_of(slot * 2, 2), 2)],
            send_sem=sum_send.at[which], recv_sem=sum_recv.at[which], device_id=target, device_id_type=MESH,
        ).start()

    for kt in range(SHARDS):
        def send_one(i, carry, kt=kt):
            ks = i ^ FAR

            def go():
                send_sums(0, (tm ^ kt, sp ^ ks), kt * TILES + ks, got1)

            if kt:
                go()
            else:
                pl.when(ks != 0)(go)
            return carry

        lax.fori_loop(0, TILES, send_one, 0)

    def piece(dr, dc):
        if dc == 0:
            return own.at[pl.ds(0, 32)] if dr < 0 else own.at[pl.ds(32, 32)]
        return side.at[0] if dc < 0 else side.at[1]

    for dt in (3, 2, 1, 0):
        @pl.when(tm + dt < SHARDS)
        def _(dt=dt):
            def push(src, at, rows, target):
                pltpu.make_async_remote_copy(
                    src_ref=src, dst_ref=hbuf.at[3 - dt, pl.ds(at, rows)], send_sem=hid_send.at[dt],
                    recv_sem=hid_recv.at[dt], device_id=target, device_id_type=MESH,
                ).start()

            for i in (4, 5, 6, 7, 0, 1, 2, 3):
                dr, dc = RING[i]
                there = ((tile_row + dr) & 7) * GRID_COLS + ((tile_col + dc) & 3)
                at = RING_AT[RING.index((-dr, -dc))]
                push(piece(dr, dc), at, RING_ROWS[i], (tm + dt, there))
            if dt:
                push(own, 0, 64, (tm + dt, sp))

    def block_copy(dt):
        ref = hbuf.at[3 - dt, pl.ds(64, 160)] if dt == 0 else hbuf.at[3 - dt]
        return pltpu.make_async_remote_copy(
            src_ref=ref, dst_ref=ref, send_sem=hid_send.at[dt], recv_sem=hid_recv.at[dt],
            device_id=(tm ^ 1, sp), device_id_type=MESH,
        )

    def sums_copy(which, buf, rows):
        ref = buf.at[pl.ds(2, rows - 2)]
        return pltpu.make_async_remote_copy(
            src_ref=ref, dst_ref=ref, send_sem=sum_send.at[which], recv_sem=sum_recv.at[which],
            device_id=(tm ^ 1, sp), device_id_type=MESH,
        )

    for dt in range(SHARDS):
        @pl.when(tm >= dt)
        def _(dt=dt):
            block_copy(dt).wait_recv()

    sums_copy(0, got1, 256).wait_recv()

    starting = tm == 0
    row8 = iota((8, LANES), 0)
    stats = []
    for dt in range(SHARDS):
        kt = tm ^ ((tm - dt) & 3)
        stats.append(group_stats(got1[pl.ds(pl.multiple_of(kt * 64, 64), 64)], TILES * 16 * 16))
    span = (0, 0, 0, 0, 1, 1, 1, 1)
    steps = (0, 1, 2, 3, 0, 1, 2, 3)
    normers = []
    for half in range(2):
        pair = []
        for which in range(2):
            rows = by_frame(stats[3 - 2 * half][which], stats[2 - 2 * half][which], span, steps)
            if half:
                rows = jnp.where(starting & (row8 < 4), jnp.broadcast_to(rows[4:5], (8, LANES)), rows)
            pair.append(spread(rows))
        normers.append((pair[0], pair[1] * gain1[...]))
    shift1 = bias1[...]
    low = iota((1, 8, C), 1) < 4

    def place(cells, parts, odd):
        halves = []
        for half in range(2):
            a, b = parts[2 * half], parts[2 * half + 1]
            if odd:
                a = sub_roll(a, 4)
            else:
                b = sub_roll(b, 4)
            halves.append(jnp.where(low, a, b))
        lo, hi = halves
        hi = jnp.where(starting & low, jnp.broadcast_to(hi[:, 4:5], hi.shape), hi)
        nlo = (lo - normers[0][0]) * normers[0][1] + shift1
        nhi = (hi - normers[1][0]) * normers[1][1] + shift1
        for i, cell in enumerate(cells):
            xhi[cell] = hi[i]
            normed[cell] = jnp.concatenate([nlo[i], nhi[i]], axis=0).astype(BF16)

    def rows_of(at, count):
        return [hbuf[s, at : at + count].astype(F32).reshape(count // 8, 8, C) for s in range(4)]

    for r in range(4):
        at = (64, 0, 32, 96)[r]
        parts = rows_of(at, 32)
        for odd in range(2):
            place([r * 10 + 1 + 2 * i + odd for i in range(4)], parts, odd)
    for i, cells in (
        (2, ((10, 0, 1), (20, 1, 1))), (3, ((19, 0, 0), (29, 1, 0))),
        (4, ((0, 1, 1),)), (5, ((9, 1, 0),)), (6, ((30, 0, 1),)), (7, ((39, 0, 0),)),
    ):
        parts = rows_of(RING_AT[i], 16)
        for cell, pair, odd in cells:
            place([cell], [p[pair : pair + 1] for p in parts], odd)

    for g in range(20):
        two = normed[2 * g : 2 * g + 2].astype(F32)
        queries[16 * g : 16 * g + 16] = jnp.concatenate([two[0, 8:16], two[1, 8:16]], axis=0).astype(BF16)
    asked = jnp.dot(queries[...], wqkv[:, 0:C], preferred_element_type=F32)
    queries[...] = asked.astype(BF16)
    everything = normed[...].reshape(CELLS * 16, C)
    keys[...] = jnp.dot(everything, wqkv[:, C : 2 * C], preferred_element_type=F32).astype(BF16)
    values[...] = jnp.dot(everything, wqkv[:, 2 * C :], preferred_element_type=F32).astype(BF16)

    q_row, k_col = iota((64, 128), 0), iota((64, 128), 1)
    first_frame = 12 - 4 * tm
    q_frame = jnp.maximum((q_row & 7) + 8, first_frame)
    k_frame = k_col & 15
    allowed = ((q_row >> 3) == (k_col >> 4)) & (k_frame <= q_frame) & (k_frame >= first_frame)
    for g in range(5):
        q = queries[64 * g : 64 * g + 64]
        k = keys[128 * g : 128 * g + 128]
        v = values[128 * g : 128 * g + 128]
        scores = lax.dot_general(q, k, (((1,), (1,)), ((), ())), preferred_element_type=F32) * C ** (-0.5)
        scores = jnp.where(allowed, scores, -1e30)
        weights = jnp.exp(scores - jnp.max(scores, axis=1, keepdims=True))
        weights = jnp.where(allowed, weights, 0.0)
        total = jnp.sum(weights, axis=1, keepdims=True)
        summed = jnp.dot(weights.astype(BF16), v, preferred_element_type=F32)
        attended[64 * g : 64 * g + 64] = (summed / total).astype(BF16)

    projected = jnp.dot(attended[...], wout[...], preferred_element_type=F32).reshape(CELLS, 8, C)
    top, bottom = tile_row == 0, tile_row == GRID_ROWS - 1
    leftmost, rightmost = tile_col == 0, tile_col == GRID_COLS - 1
    for r in range(4):
        mixed = (xhi[10 * r : 10 * r + 10] + (projected[10 * r : 10 * r + 10] + bout[...])).astype(BF16).astype(F32)
        col = iota((10, 8, C), 0)
        outside = (leftmost & (col == 0)) | (rightmost & (col == 9))
        if r == 0:
            outside = outside | top
        if r == 3:
            outside = outside | bottom
        mixed = jnp.where(outside, 0.0, mixed)
        for a in range(3):
            moved = sub_roll(mixed, -a) if a else mixed
            mixcat[80 * r : 80 * r + 80, a * C : (a + 1) * C] = moved.reshape(80, C).astype(BF16)

    def wait_first(i, carry):
        tap_copies(i)[0].wait()
        return carry

    lax.fori_loop(0, 27, wait_first, 0)

    def first_taps(e, carry):
        for b in range(3):
            begin, end = ((0, 240), (0, 320), (80, 320))[b]
            t1[b, e, begin:end] = jnp.dot(mixcat[begin:end], w1[3 * b + e], preferred_element_type=F32)
        return carry

    lax.fori_loop(0, 3, first_taps, 0)

    def t1_row(b, e, r, lanes):
        return t1[b, e, 80 * r : 80 * r + 80, lanes].reshape(10, 8, LANES)

    sum_first, sum_second = [], []
    for k in range(CHUNKS):
        lanes = slice(k * LANES, (k + 1) * LANES)
        acc, acc2 = jnp.zeros((8, LANES), F32), jnp.zeros((8, LANES), F32)
        for R in range(6):
            s = []
            for e in range(3):
                if R % 2 == 0:
                    r = R // 2
                    s.append(t1_row(0, e, r, lanes) + t1_row(1, e, r, lanes) + t1_row(2, e, r + 1, lanes))
                else:
                    r = (R + 1) // 2
                    s.append(t1_row(0, e, r - 1, lanes) + t1_row(1, e, r, lanes) + t1_row(2, e, r, lanes))
            even = s[0][0:9] + s[1][0:9] + s[2][1:10] + b1[:, lanes]
            odd = s[0][0:9] + s[1][1:10] + s[2][1:10] + b1[:, lanes]
            even = even.astype(BF16).astype(F32)
            odd = odd.astype(BF16).astype(F32)
            fs[R, 0, :, :, lanes] = even
            fs[R, 1, :, :, lanes] = odd
            if 1 <= R <= 4:
                inner_e, inner_o = even[1:9], odd[0:8]
                acc = acc + jnp.sum(inner_e, axis=0) + jnp.sum(inner_o, axis=0)
                acc2 = acc2 + jnp.sum(inner_e * inner_e, axis=0) + jnp.sum(inner_o * inner_o, axis=0)
        sum_first.append(acc)
        sum_second.append(acc2)
    packed = jnp.concatenate(
        [pack_sums(jnp.concatenate(sum_first, axis=1), 2), pack_sums(jnp.concatenate(sum_second, axis=1), 2)], axis=0
    )
    sums[1] = packed
    got2[0:2] = packed

    def send_second(i, carry):
        ks = i ^ FAR
        send_sums(1, ((tm + 1) & 3, sp ^ ks), TILES + ks, got2)

        @pl.when(ks != 0)
        def _():
            send_sums(1, (tm, sp ^ ks), ks, got2)

        return carry

    lax.fori_loop(0, TILES, send_second, 0)

    def wait_second(i, carry):
        tap_copies(i)[1].wait()
        return carry

    lax.fori_loop(0, 27, wait_second, 0)
    sums_copy(1, got2, 128).wait_recv()

    stats_own = group_stats(got2[0:64], TILES * 64 * 16)
    stats_before = group_stats(got2[64:128], TILES * 64 * 16)
    pair = []
    for which in range(2):
        rows = by_frame(stats_before[which], stats_own[which], (0, 0, 1, 1, 1, 1, 1, 1), (2, 3, 0, 1, 2, 3, 3, 3))
        rows = jnp.where(starting & (row8 < 2), jnp.broadcast_to(rows[2:3], (8, LANES)), rows)
        pair.append(spread(rows))
    mean2, scale2 = pair[0], pair[1] * gain2[...]
    low4 = iota((1, 8, LANES), 1) < 4
    index9 = iota((9, 8, LANES), 0)
    for R in range(6):
        for k in range(CHUNKS):
            lanes = slice(k * LANES, (k + 1) * LANES)
            both = []
            for parity in range(2):
                v = (fs[R, parity, :, :, lanes] - mean2[:, lanes]) * scale2[:, lanes] + bias2[:, lanes]
                v = 0.5 * v * (1.0 + jnp.tanh(0.5 * v))
                outside = (rightmost & (index9 == 8)) if parity else (leftmost & (index9 == 0))
                if R == 0:
                    outside = outside | top
                if R == 5:
                    outside = outside | bottom
                both.append(jnp.where(outside, 0.0, v))
            for a in range(3):
                joined = []
                for parity in range(2):
                    lower, upper = both[parity][0:5], both[parity][4:9]
                    lower = sub_roll(lower, -a) if a else lower
                    joined.append(jnp.where(low4, lower, sub_roll(upper, 4 - a)))
                tile = jnp.concatenate(joined, axis=1).reshape(80, LANES).astype(BF16)
                actcat[80 * R : 80 * R + 80, a * C + k * LANES : a * C + (k + 1) * LANES] = tile

    def second_taps(e, carry):
        for b in range(3):
            begin, end = ((0, 400), (80, 400), (80, 480))[b]
            t2[b, e, begin:end] = jnp.dot(actcat[begin:end], w2[3 * b + e], preferred_element_type=F32)
        return carry

    lax.fori_loop(0, 3, second_taps, 0)

    to, fro = iota((128, 128), 0), iota((128, 128), 1)
    place_f, place_col = to >> 5, to & 31
    j = place_col >> 1
    source = (place_col & 1) * 64 + (j & 7) * 8 + (j >> 3) * 4 + place_f
    shuffle = jnp.where(fro == source, 1.0, 0.0).astype(BF16)
    for row in range(8):
        R = row // 2 + 1
        s = []
        for e in range(3):
            picks = (R - 1, R, R) if row % 2 == 0 else (R, R, R + 1)
            terms = [t2[b, e, 80 * at : 80 * at + 80].reshape(10, 8, C2) for b, at in enumerate(picks)]
            s.append(terms[0] + terms[1] + terms[2])
        q0 = s[0][0:8] + s[1][1:9] + s[2][1:9] + b2[...]
        q1 = s[0][1:9] + s[1][1:9] + s[2][2:10] + b2[...]
        stacked = jnp.concatenate([q0.reshape(64, C2), q1.reshape(64, C2)], axis=0).astype(BF16)
        final = jnp.dot(shuffle, stacked, preferred_element_type=F32).astype(BF16)
        for f in range(FRAMES):
            out_ref[f, row] = final[32 * f : 32 * f + 32]

    for dt in range(SHARDS):
        @pl.when(tm + dt < SHARDS)
        def _(dt=dt):
            block_copy(dt).wait_send()
    sums_copy(0, got1, 256).wait_send()
    sums_copy(1, got2, 128).wait_send()


def per_device(
    hidden_state, norm1_gain, norm1_bias, qkv_weight, out_weight, out_bias, conv1_weight, conv1_bias,
    norm2_gain, norm2_bias, conv2_weight, conv2_bias,
):
    any_spec = pl.BlockSpec(memory_space=pl.ANY)
    decoded = pl.pallas_call(
        kernel,
        out_shape=jax.ShapeDtypeStruct((FRAMES, 8, 32, C2), BF16),
        in_specs=[any_spec] * 12,
        out_specs=pl.BlockSpec(memory_space=pltpu.VMEM),
        scratch_shapes=[
            pltpu.VMEM((FRAMES, 2, 8, C), BF16),
            pltpu.VMEM((1, C), F32),
            pltpu.VMEM((1, C), F32),
            pltpu.VMEM((C, 3 * C), BF16),
            pltpu.VMEM((C, C), BF16),
            pltpu.VMEM((1, C), F32),
            pltpu.VMEM((9, 3 * C, C), BF16),
            pltpu.VMEM((1, C), F32),
            pltpu.VMEM((1, C), F32),
            pltpu.VMEM((1, C), F32),
            pltpu.VMEM((9, 3 * C, C2), BF16),
            pltpu.VMEM((1, C2), F32),
            pltpu.VMEM((64, C), BF16),
            pltpu.VMEM((2, 16, C), BF16),
            pltpu.VMEM((4, BLOCK_ROWS, C), BF16),
            pltpu.VMEM((2, 2, LANES), F32),
            pltpu.VMEM((256, LANES), F32),
            pltpu.VMEM((128, LANES), F32),
            pltpu.VMEM((CELLS, 8, C), F32),
            pltpu.VMEM((CELLS, 16, C), BF16),
            pltpu.VMEM((CELLS * 8, C), BF16),
            pltpu.VMEM((CELLS * 16, C), BF16),
            pltpu.VMEM((CELLS * 16, C), BF16),
            pltpu.VMEM((CELLS * 8, C), BF16),
            pltpu.VMEM((CELLS * 8, 3 * C), BF16),
            pltpu.VMEM((3, 3, CELLS * 8, C), F32),
            pltpu.VMEM((6, 2, 9, 8, C), F32),
            pltpu.VMEM((480, 3 * C), BF16),
            pltpu.VMEM((3, 3, 480, C2), F32),
            pltpu.SemaphoreType.DMA((10,)),
            pltpu.SemaphoreType.DMA((27,)),
            pltpu.SemaphoreType.DMA((27,)),
            pltpu.SemaphoreType.DMA((SHARDS,)),
            pltpu.SemaphoreType.DMA((SHARDS,)),
            pltpu.SemaphoreType.DMA((2,)),
            pltpu.SemaphoreType.DMA((2,)),
        ],
        compiler_params=pltpu.CompilerParams(collective_id=0, has_side_effects=True, vmem_limit_bytes=60 << 20),
    )(
        hidden_state.reshape(FRAMES, 2, 8, C),
        norm1_gain.reshape(1, C),
        norm1_bias.reshape(1, C),
        qkv_weight,
        out_weight,
        out_bias.reshape(1, C),
        conv1_weight.reshape(27, C, C),
        conv1_bias.reshape(1, C),
        norm2_gain.reshape(1, C),
        norm2_bias.reshape(1, C),
        conv2_weight.reshape(27, C, C2),
        conv2_bias.reshape(1, C2),
    )
    return decoded[:, None]


def solution(mesh):
    return jax.shard_map(
        per_device,
        mesh=mesh,
        in_specs=(P("tm", "space", None, None, None),) + (P(),) * 11,
        out_specs=P("tm", "space", None, None, None),
        check_vma=False,
    )
```

time: 334 us -> 52.5 us (0.16)
  blocking collectives: 190 us -> 0 us
  local copies, waits for them, and re-layouts: 61.4 us -> 1.87 us
  Pallas kernels: 0 us -> 50.5 us
  starting transfers between devices: 34.1 us -> 0 us
  other arithmetic: 16.6 us -> 0 us
  matrix products: 15.2 us -> 0 us
  waiting for transfers between devices: 12.9 us -> 0 us
    psum x2 -> x0, blocking collectives: 164 us -> none  [frame_norm(): first_sum, second_sum = lax.psum((first_sum, second_sum), 'space')]
    pallas_call x0 -> x1, Pallas kernels: none -> 50.5 us  [per_device(): pl.pallas_call(kernel, out_shape=jax.ShapeDtypeStruct((FRAMES, 8, 32, C2)...]
    ppermute x10 -> x0, starting transfers between devices: 34.1 us -> none  [shifted(): lax.ppermute(value, axis, [(source, source + steps) for source in range(l...]
    slice x12 -> x0, local copies, waits for them, and re-layouts: 31.7 us -> none  [the longest x4 16.5 us: upsample_conv(): upsampled[time_offset:time_offset + frames, row_offset:row_offset + 2 * h...]
    all_gather x2 -> x0, blocking collectives: 26.2 us -> none  [the longest x1 20.3 us: gathered_attention(): key_piece = lax.all_gather(keys, 'tm', axis=0, tiled=True)]
    dot_general x22 -> x0, matrix products: 15.2 us -> none  [the longest x18 13.9 us: upsample_conv(): jnp.dot(slab, weight[time_offset, row_offset].reshape(3 * chans, outs), p...]
    ppermute x10 -> x0, waiting for transfers between devices: 12.9 us -> none  [shifted(): lax.ppermute(value, axis, [(source, source + steps) for source in range(l...]
    reshape x3 -> x0, local copies, waits for them, and re-layouts: 10.4 us -> none  [the longest x1 5.63 us: upsample_conv(): jnp.repeat(jnp.repeat(extended, 2, axis=1), 2, axis=2)[:, 1:-1, 1:-1]]
  transfers between devices with their start and end apart: 10 -> 0, of which waited for: 4 -> 0; matrix products, arithmetic and copies ran while one was open for 5% -> 0% of each run, Pallas kernels for 0% -> 0%
where the time goes in v1:
time: 52.5 us; the launch traced here: 52.3 us
  Pallas kernels  50.5 us (96%)
  local copies, waits for them, and re-layouts  1.87 us (4%)
    pallas_call x1, Pallas kernels, per_device(): pl.pallas_call(kernel, out_shape=jax.ShapeDtypeStruct((FRAMES, 8, 32, C2)...  50.5 us
    unnamed x1, local copies, waits for them, and re-layouts  1.87 us

profile of v1, /device:TPU:1, one launch (start us, length us, event | category | flops | bytes accessed | tf_op | source)
XLA Modules:
  0.0 52.3 jit_solution(4940067224199803176)
XLA Ops:
  0.0 50.5 %shard_map.118 = bf16[4,8,32,256]{3,2,1,0:T(8,128)(2,1)} custom-call(bf16[4,2,8,512]{3,2,1,0:T(8,128)(2,1)} %bitcast.16, f32[1,512]{1,0:T(1,128)} %bitcast.17, f32[1,512]{1,0:T(1,128)} %bitcast.18, bf16[512,1536]{1,0:T(8,128)(2,1)} %wqkv_hbm.1, bf16[512,512]{1,0:T(8,128)(2,1)} %wout_hbm.1, f32[1,512]{1,0:T(1,128)} %bitcast.19, ...), custom_call_target="tpu_custom_call" | custom-call | tf_op jit(solution)/shard_map/pallas_call | solution.py:467
  50.5 1.9 %copy.15 = bf16[4,1,8,32,256]{4,3,2,1,0:T(8,128)(2,1)} copy(bf16[4,1,8,32,256]{4,3,2,1,0:T(8,128)(2,1)} %bitcast.15) | data formatting | bytes 1048576

commit v2 on v1

--- a/solution.py
+++ b/solution.py
@@ -12,12 +12,17 @@
 GRID_COLS, GRID_ROWS, TILES, SHARDS = 4, 8, 32, 4
 FRAMES = 4
 CELLS = 40
-FAR = 21
+
+def hops(kt, ks):
+    return sum((0, 1, 2, 1)[v] for v in (ks >> 3, (ks >> 1) & 3, (ks & 1) * 2 + (kt >> 1)))
+
+
+PEERS = sorted(((kt, ks) for kt in range(SHARDS) for ks in range(TILES) if kt or ks), key=lambda p: -hops(*p))
 EPS = 1e-6
-RING = ((-1, 0), (1, 0), (0, -1), (0, 1), (-1, -1), (-1, 1), (1, -1), (1, 1))
-RING_ROWS = (32, 32, 16, 16, 16, 16, 16, 16)
-RING_AT = (64, 96, 128, 144, 160, 176, 192, 208)
-BLOCK_ROWS = 224
+RING = ((-1, -1), (-1, 1), (1, -1), (1, 1), (-1, 0), (1, 0), (0, -1), (0, 1))
+RING_ROWS = (16, 16, 16, 16, 128, 128, 32, 32)
+RING_AT = (576, 592, 608, 624, 256, 384, 512, 544)
+BLOCK_ROWS = 640
 
 
 def iota(shape, axis):
@@ -30,6 +35,13 @@
 
 def sub_roll(value, shift):
     return pltpu.roll(value, shift % 8, axis=value.ndim - 2)
+
+
+def by_chunk(value, rows):
+    parts = [
+        value[i : i + rows, k * LANES : (k + 1) * LANES] for i in range(0, value.shape[0], rows) for k in range(CHUNKS)
+    ]
+    return jnp.concatenate(parts, axis=0)
 
 
 def pack_sums(total, first_row):
@@ -84,8 +96,8 @@
     hid_hbm, gain1_hbm, bias1_hbm, wqkv_hbm, wout_hbm, bout_hbm, w1_hbm, b1_hbm, gain2_hbm, bias2_hbm, w2_hbm, b2_hbm,
     out_ref,
     hid, gain1, bias1, wqkv, wout, bout, w1, b1, gain2, bias2, w2, b2,
-    own, side, hbuf, sums, got1, got2, xhi, normed, queries, keys, values, attended, mixcat, t1, fs, actcat, t2,
-    small_sem, w1_sem, w2_sem, hid_send, hid_recv, sum_send, sum_recv,
+    side, hbuf, sums, got1, got2, xhi, normed, queries, keys, values, attended, mixcat, t1, fs, actcat, t2,
+    small_sem, w1_sem, w2_sem, hid_send, hid_recv, pass_send, sum_send, sum_recv,
 ):
     tm = lax.axis_index("tm")
     sp = lax.axis_index("space")
@@ -104,20 +116,8 @@
         copy.start()
 
     barrier = pltpu.get_barrier_semaphore()
-    for kt in range(SHARDS):
-        def greet(i, carry, kt=kt):
-            ks = i ^ FAR
-
-            def signal():
-                pl.semaphore_signal(barrier, inc=1, device_id=(tm ^ kt, sp ^ ks), device_id_type=MESH)
-
-            if kt:
-                signal()
-            else:
-                pl.when(ks != 0)(signal)
-            return carry
-
-        lax.fori_loop(0, TILES, greet, 0)
+    for kt, ks in PEERS:
+        pl.semaphore_signal(barrier, inc=1, device_id=(tm ^ kt, sp ^ ks), device_id_type=MESH)
 
     def tap_copies(i):
         a, be = i // 9, lax.rem(i, 9)
@@ -141,7 +141,7 @@
     for dt in range(1, SHARDS):
         @pl.when(tm < dt)
         def _():
-            hbuf[3 - dt] = jnp.zeros((BLOCK_ROWS, C), BF16)
+            hbuf[3 - dt] = jnp.zeros((BLOCK_ROWS, LANES), BF16)
 
     for copy in smalls:
         copy.wait()
@@ -150,11 +150,19 @@
     permute = jnp.where(order_in == wanted, 1.0, 0.0).astype(BF16)
     plain = hid[...].astype(F32).reshape(64, C).astype(BF16)
     mine = jnp.dot(permute, plain, preferred_element_type=F32)
-    mine16 = mine.astype(BF16)
-    own[...] = mine16
-    hbuf[3, 0:64] = mine16
-    side[0] = jnp.concatenate([mine[0:8], mine[32:40]], axis=0).astype(BF16)
-    side[1] = jnp.concatenate([mine[24:32], mine[56:64]], axis=0).astype(BF16)
+    hbuf[3, 0:256] = by_chunk(mine, 32).astype(BF16)
+    low2 = iota((8, LANES), 0) < 4
+    edges = (
+        jnp.where(iota((8, C), 0) < 4, mine[0:8], sub_roll(mine[32:40], 4)),
+        jnp.where(iota((8, C), 0) < 4, sub_roll(mine[24:32], 4), mine[56:64]),
+    )
+    for i, edge in enumerate(edges):
+        side[32 * i : 32 * i + 32] = by_chunk(edge, 8).astype(BF16)
+        chunk = [edge[:, k * LANES : (k + 1) * LANES] for k in range(CHUNKS)]
+        upper = [jnp.where(low2, chunk[k], sub_roll(chunk[k + 1], 4)) for k in (0, 2)]
+        lower = [jnp.where(low2, sub_roll(chunk[k], 4), chunk[k + 1]) for k in (0, 2)]
+        side[64 + 16 * i : 80 + 16 * i] = jnp.concatenate(upper, axis=0).astype(BF16)
+        side[96 + 16 * i : 112 + 16 * i] = jnp.concatenate(lower, axis=0).astype(BF16)
     pairs = mine.reshape(8, 8, C)
     first = jnp.sum(pairs, axis=0)
     second = jnp.sum(pairs * pairs, axis=0)
@@ -172,48 +180,44 @@
             send_sem=sum_send.at[which], recv_sem=sum_recv.at[which], device_id=target, device_id_type=MESH,
         ).start()
 
-    for kt in range(SHARDS):
-        def send_one(i, carry, kt=kt):
-            ks = i ^ FAR
-
-            def go():
-                send_sums(0, (tm ^ kt, sp ^ ks), kt * TILES + ks, got1)
-
-            if kt:
-                go()
-            else:
-                pl.when(ks != 0)(go)
-            return carry
-
-        lax.fori_loop(0, TILES, send_one, 0)
+    for kt, ks in PEERS:
+        send_sums(0, (tm ^ kt, sp ^ ks), kt * TILES + ks, got1)
 
     def piece(dr, dc):
         if dc == 0:
-            return own.at[pl.ds(0, 32)] if dr < 0 else own.at[pl.ds(32, 32)]
-        return side.at[0] if dc < 0 else side.at[1]
-
-    for dt in (3, 2, 1, 0):
-        @pl.when(tm + dt < SHARDS)
-        def _(dt=dt):
-            def push(src, at, rows, target):
-                pltpu.make_async_remote_copy(
-                    src_ref=src, dst_ref=hbuf.at[3 - dt, pl.ds(at, rows)], send_sem=hid_send.at[dt],
-                    recv_sem=hid_recv.at[dt], device_id=target, device_id_type=MESH,
-                ).start()
-
-            for i in (4, 5, 6, 7, 0, 1, 2, 3):
-                dr, dc = RING[i]
-                there = ((tile_row + dr) & 7) * GRID_COLS + ((tile_col + dc) & 3)
-                at = RING_AT[RING.index((-dr, -dc))]
-                push(piece(dr, dc), at, RING_ROWS[i], (tm + dt, there))
-            if dt:
-                push(own, 0, 64, (tm + dt, sp))
+            return hbuf.at[3, pl.ds(0, 128)] if dr < 0 else hbuf.at[3, pl.ds(128, 128)]
+        column = 0 if dc < 0 else 1
+        if dr == 0:
+            return side.at[pl.ds(32 * column, 32)]
+        return side.at[pl.ds((64 if dr < 0 else 96) + 16 * column, 16)]
+
+    def ring_push(dt):
+        def push(src, at, rows, target):
+            pltpu.make_async_remote_copy(
+                src_ref=src, dst_ref=hbuf.at[3 - dt, pl.ds(at, rows)], send_sem=hid_send.at[dt],
+                recv_sem=hid_recv.at[dt], device_id=target, device_id_type=MESH,
+            ).start()
+
+        for i, (dr, dc) in enumerate(RING):
+            there = ((tile_row + dr) & 7) * GRID_COLS + ((tile_col + dc) & 3)
+            push(piece(dr, dc), RING_AT[RING.index((-dr, -dc))], RING_ROWS[i], (tm + dt, there))
+        if dt:
+            push(hbuf.at[3, pl.ds(0, 256)], 0, 256, (tm + dt, sp))
+
+    ring_push(0)
+    pl.when(tm < 2)(lambda: ring_push(2))
 
     def block_copy(dt):
-        ref = hbuf.at[3 - dt, pl.ds(64, 160)] if dt == 0 else hbuf.at[3 - dt]
+        ref = hbuf.at[3, pl.ds(256, 384)] if dt == 0 else hbuf.at[3 - dt]
         return pltpu.make_async_remote_copy(
             src_ref=ref, dst_ref=ref, send_sem=hid_send.at[dt], recv_sem=hid_recv.at[dt],
             device_id=(tm ^ 1, sp), device_id_type=MESH,
+        )
+
+    def forward(here, there):
+        return pltpu.make_async_remote_copy(
+            src_ref=hbuf.at[3 - here], dst_ref=hbuf.at[3 - there], send_sem=pass_send.at[here // 2],
+            recv_sem=hid_recv.at[there], device_id=(tm ^ 1, sp), device_id_type=MESH,
         )
 
     def sums_copy(which, buf, rows):
@@ -223,10 +227,18 @@
             device_id=(tm ^ 1, sp), device_id_type=MESH,
         )
 
-    for dt in range(SHARDS):
-        @pl.when(tm >= dt)
-        def _(dt=dt):
-            block_copy(dt).wait_recv()
+    first_core = (tm & 1) == 0
+    block_copy(0).wait_recv()
+    pl.when(first_core)(lambda: forward(0, 1).start())
+
+    @pl.when(tm >= 2)
+    def _():
+        block_copy(2).wait_recv()
+        pl.when(first_core)(lambda: forward(2, 3).start())
+        pl.when(jnp.logical_not(first_core))(lambda: forward(2, 1).start())
+
+    pl.when(tm >= 1)(lambda: block_copy(1).wait_recv())
+    pl.when(tm == 3)(lambda: block_copy(3).wait_recv())
 
     sums_copy(0, got1, 256).wait_recv()
 
@@ -267,21 +279,33 @@
             xhi[cell] = hi[i]
             normed[cell] = jnp.concatenate([nlo[i], nhi[i]], axis=0).astype(BF16)
 
-    def rows_of(at, count):
-        return [hbuf[s, at : at + count].astype(F32).reshape(count // 8, 8, C) for s in range(4)]
+    def rows_of(at, rows):
+        out = []
+        for s in range(4):
+            value = hbuf[s, at : at + CHUNKS * rows].astype(F32)
+            value = jnp.concatenate([value[k * rows : (k + 1) * rows] for k in range(CHUNKS)], axis=1)
+            out.append(value.reshape(rows // 8, 8, C))
+        return out
+
+    def corner_of(at):
+        out = []
+        for s in range(4):
+            value = hbuf[s, at : at + 16].astype(F32)
+            halves = (value[0:8], value[8:16])
+            value = jnp.concatenate([sub_roll(halves[k // 2], 4 * (k & 1)) if k & 1 else halves[k // 2] for k in range(CHUNKS)], axis=1)
+            out.append(value.reshape(1, 8, C))
+        return out
 
     for r in range(4):
-        at = (64, 0, 32, 96)[r]
-        parts = rows_of(at, 32)
+        parts = rows_of((256, 0, 128, 384)[r], 32)
         for odd in range(2):
             place([r * 10 + 1 + 2 * i + odd for i in range(4)], parts, odd)
-    for i, cells in (
-        (2, ((10, 0, 1), (20, 1, 1))), (3, ((19, 0, 0), (29, 1, 0))),
-        (4, ((0, 1, 1),)), (5, ((9, 1, 0),)), (6, ((30, 0, 1),)), (7, ((39, 0, 0),)),
-    ):
-        parts = rows_of(RING_AT[i], 16)
-        for cell, pair, odd in cells:
-            place([cell], [p[pair : pair + 1] for p in parts], odd)
+    for at, column in ((512, 0), (544, 9)):
+        parts = rows_of(at, 8)
+        place([10 + column], parts, 0)
+        place([20 + column], parts, 1)
+    for i, cell in enumerate((0, 9, 30, 39)):
+        place([cell], corner_of(RING_AT[i]), 0)
 
     for g in range(20):
         two = normed[2 * g : 2 * g + 2].astype(F32)
@@ -373,17 +397,11 @@
     sums[1] = packed
     got2[0:2] = packed
 
-    def send_second(i, carry):
-        ks = i ^ FAR
-        send_sums(1, ((tm + 1) & 3, sp ^ ks), TILES + ks, got2)
-
-        @pl.when(ks != 0)
-        def _():
+    for kt, ks in PEERS:
+        if kt == 0:
             send_sums(1, (tm, sp ^ ks), ks, got2)
-
-        return carry
-
-    lax.fori_loop(0, TILES, send_second, 0)
+        if kt == 1:
+            send_sums(1, ((tm + 1) & 3, sp ^ ks), TILES + ks, got2)
 
     def wait_second(i, carry):
         tap_copies(i)[1].wait()
@@ -451,10 +469,10 @@
         for f in range(FRAMES):
             out_ref[f, row] = final[32 * f : 32 * f + 32]
 
-    for dt in range(SHARDS):
-        @pl.when(tm + dt < SHARDS)
-        def _(dt=dt):
-            block_copy(dt).wait_send()
+    block_copy(0).wait_send()
+    pl.when(tm < 2)(lambda: block_copy(2).wait_send())
+    pl.when(first_core)(lambda: forward(0, 1).wait_send())
+    pl.when(tm >= 2)(lambda: forward(2, 1).wait_send())
     sums_copy(0, got1, 256).wait_send()
     sums_copy(1, got2, 128).wait_send()
 
@@ -482,9 +500,8 @@
             pltpu.VMEM((1, C), F32),
             pltpu.VMEM((9, 3 * C, C2), BF16),
             pltpu.VMEM((1, C2), F32),
-            pltpu.VMEM((64, C), BF16),
-            pltpu.VMEM((2, 16, C), BF16),
-            pltpu.VMEM((4, BLOCK_ROWS, C), BF16),
+            pltpu.VMEM((128, LANES), BF16),
+            pltpu.VMEM((4, BLOCK_ROWS, LANES), BF16),
             pltpu.VMEM((2, 2, LANES), F32),
             pltpu.VMEM((256, LANES), F32),
             pltpu.VMEM((128, LANES), F32),
@@ -506,6 +523,7 @@
             pltpu.SemaphoreType.DMA((SHARDS,)),
             pltpu.SemaphoreType.DMA((2,)),
             pltpu.SemaphoreType.DMA((2,)),
+            pltpu.SemaphoreType.DMA((2,)),
         ],
         compiler_params=pltpu.CompilerParams(collective_id=0, has_side_effects=True, vmem_limit_bytes=60 << 20),
     )(

time: 52.5 us -> 41.1 us (0.78)
  Pallas kernels: 50.5 us -> 39 us
    pallas_call x1, Pallas kernels: 50.5 us -> 39 us  [per_device(): pl.pallas_call(kernel, out_shape=jax.ShapeDtypeStruct((FRAMES, 8, 32, C2)...]
where the time goes in v2:
time: 41.1 us; the launch traced here: 40.9 us
  Pallas kernels  39 us (95%)
  local copies, waits for them, and re-layouts  1.87 us (5%)
    pallas_call x1, Pallas kernels, per_device(): pl.pallas_call(kernel, out_shape=jax.ShapeDtypeStruct((FRAMES, 8, 32, C2)...  39 us
    unnamed x1, local copies, waits for them, and re-layouts  1.87 us

profile of v2, /device:TPU:1, one launch (start us, length us, event | category | flops | bytes accessed | tf_op | source)
XLA Modules:
  0.0 40.9 jit_solution(14730689049077945495)
XLA Ops:
  0.0 39.0 %shard_map.118 = bf16[4,8,32,256]{3,2,1,0:T(8,128)(2,1)} custom-call(bf16[4,2,8,512]{3,2,1,0:T(8,128)(2,1)} %bitcast.16, f32[1,512]{1,0:T(1,128)} %bitcast.17, f32[1,512]{1,0:T(1,128)} %bitcast.18, bf16[512,1536]{1,0:T(8,128)(2,1)} %wqkv_hbm.1, bf16[512,512]{1,0:T(8,128)(2,1)} %wout_hbm.1, f32[1,512]{1,0:T(1,128)} %bitcast.19, ...), custom_call_target="tpu_custom_call" | custom-call | tf_op jit(solution)/shard_map/pallas_call | solution.py:485
  39.0 1.9 %copy.15 = bf16[4,1,8,32,256]{4,3,2,1,0:T(8,128)(2,1)} copy(bf16[4,1,8,32,256]{4,3,2,1,0:T(8,128)(2,1)} %bitcast.15) | data formatting | bytes 1048576

commit v3 on v2

--- a/solution.py
+++ b/solution.py
@@ -97,7 +97,7 @@
     out_ref,
     hid, gain1, bias1, wqkv, wout, bout, w1, b1, gain2, bias2, w2, b2,
     side, hbuf, sums, got1, got2, xhi, normed, queries, keys, values, attended, mixcat, t1, fs, actcat, t2,
-    small_sem, w1_sem, w2_sem, hid_send, hid_recv, pass_send, sum_send, sum_recv,
+    small_sem, w1_sem, w2_sem, hid_send, hid_recv, pass_send, cen_send, cen_recv, cpass_send, sum_send, sum_recv,
 ):
     tm = lax.axis_index("tm")
     sp = lax.axis_index("space")
@@ -201,24 +201,36 @@
         for i, (dr, dc) in enumerate(RING):
             there = ((tile_row + dr) & 7) * GRID_COLS + ((tile_col + dc) & 3)
             push(piece(dr, dc), RING_AT[RING.index((-dr, -dc))], RING_ROWS[i], (tm + dt, there))
-        if dt:
-            push(hbuf.at[3, pl.ds(0, 256)], 0, 256, (tm + dt, sp))
 
     ring_push(0)
     pl.when(tm < 2)(lambda: ring_push(2))
 
+    RING_PART, CENTRE = pl.ds(256, 384), pl.ds(0, 256)
+
     def block_copy(dt):
-        ref = hbuf.at[3, pl.ds(256, 384)] if dt == 0 else hbuf.at[3 - dt]
+        ref = hbuf.at[3 - dt, RING_PART]
         return pltpu.make_async_remote_copy(
             src_ref=ref, dst_ref=ref, send_sem=hid_send.at[dt], recv_sem=hid_recv.at[dt],
             device_id=(tm ^ 1, sp), device_id_type=MESH,
         )
 
-    def forward(here, there):
+    def centre_copy(dt):
         return pltpu.make_async_remote_copy(
-            src_ref=hbuf.at[3 - here], dst_ref=hbuf.at[3 - there], send_sem=pass_send.at[here // 2],
-            recv_sem=hid_recv.at[there], device_id=(tm ^ 1, sp), device_id_type=MESH,
+            src_ref=hbuf.at[3, CENTRE], dst_ref=hbuf.at[3 - dt, CENTRE], send_sem=cen_send.at[dt],
+            recv_sem=cen_recv.at[dt], device_id=(tm + dt, sp), device_id_type=MESH,
         )
+
+    def forward(here, there, part, sends, recvs):
+        return pltpu.make_async_remote_copy(
+            src_ref=hbuf.at[3 - here, part], dst_ref=hbuf.at[3 - there, part], send_sem=sends.at[here // 2],
+            recv_sem=recvs.at[there], device_id=(tm ^ 1, sp), device_id_type=MESH,
+        )
+
+    def ring_forward(here, there):
+        return forward(here, there, RING_PART, pass_send, hid_recv)
+
+    def centre_forward(here, there):
+        return forward(here, there, CENTRE, cpass_send, cen_recv)
 
     def sums_copy(which, buf, rows):
         ref = buf.at[pl.ds(2, rows - 2)]
@@ -227,19 +239,22 @@
             device_id=(tm ^ 1, sp), device_id_type=MESH,
         )
 
+    def pass_on(copy_in, passing):
+        @pl.when(tm >= 2)
+        def _():
+            copy_in(2).wait_recv()
+            pl.when(first_core)(lambda: passing(2, 3).start())
+            pl.when(jnp.logical_not(first_core))(lambda: passing(2, 1).start())
+
+    def await_passed(copy_in):
+        pl.when(tm >= 1)(lambda: copy_in(1).wait_recv())
+        pl.when(tm == 3)(lambda: copy_in(3).wait_recv())
+
     first_core = (tm & 1) == 0
-    block_copy(0).wait_recv()
-    pl.when(first_core)(lambda: forward(0, 1).start())
-
-    @pl.when(tm >= 2)
-    def _():
-        block_copy(2).wait_recv()
-        pl.when(first_core)(lambda: forward(2, 3).start())
-        pl.when(jnp.logical_not(first_core))(lambda: forward(2, 1).start())
-
-    pl.when(tm >= 1)(lambda: block_copy(1).wait_recv())
-    pl.when(tm == 3)(lambda: block_copy(3).wait_recv())
-
+    pl.when(tm < 2)(lambda: centre_copy(2).start())
+    pl.when(first_core)(lambda: centre_forward(0, 1).start())
+    pass_on(centre_copy, centre_forward)
+    await_passed(centre_copy)
     sums_copy(0, got1, 256).wait_recv()
 
     starting = tm == 0
@@ -296,48 +311,74 @@
             out.append(value.reshape(1, 8, C))
         return out
 
-    for r in range(4):
-        parts = rows_of((256, 0, 128, 384)[r], 32)
+    def line(at, cell):
+        parts = rows_of(at, 32)
         for odd in range(2):
-            place([r * 10 + 1 + 2 * i + odd for i in range(4)], parts, odd)
-    for at, column in ((512, 0), (544, 9)):
-        parts = rows_of(at, 8)
-        place([10 + column], parts, 0)
-        place([20 + column], parts, 1)
-    for i, cell in enumerate((0, 9, 30, 39)):
-        place([cell], corner_of(RING_AT[i]), 0)
-
-    for g in range(20):
-        two = normed[2 * g : 2 * g + 2].astype(F32)
-        queries[16 * g : 16 * g + 16] = jnp.concatenate([two[0, 8:16], two[1, 8:16]], axis=0).astype(BF16)
-    asked = jnp.dot(queries[...], wqkv[:, 0:C], preferred_element_type=F32)
-    queries[...] = asked.astype(BF16)
-    everything = normed[...].reshape(CELLS * 16, C)
-    keys[...] = jnp.dot(everything, wqkv[:, C : 2 * C], preferred_element_type=F32).astype(BF16)
-    values[...] = jnp.dot(everything, wqkv[:, 2 * C :], preferred_element_type=F32).astype(BF16)
+            place([cell + 2 * i + odd for i in range(4)], parts, odd)
+
+    def project(begin, end):
+        for g in range(begin // 2, end // 2):
+            two = normed[2 * g : 2 * g + 2].astype(F32)
+            queries[16 * g : 16 * g + 16] = jnp.concatenate([two[0, 8:16], two[1, 8:16]], axis=0).astype(BF16)
+        asking, rows = slice(8 * begin, 8 * end), slice(16 * begin, 16 * end)
+        queries[asking] = jnp.dot(queries[asking], wqkv[:, 0:C], preferred_element_type=F32).astype(BF16)
+        part = normed[begin:end].reshape((end - begin) * 16, C)
+        keys[rows] = jnp.dot(part, wqkv[:, C : 2 * C], preferred_element_type=F32).astype(BF16)
+        values[rows] = jnp.dot(part, wqkv[:, 2 * C :], preferred_element_type=F32).astype(BF16)
 
     q_row, k_col = iota((64, 128), 0), iota((64, 128), 1)
     first_frame = 12 - 4 * tm
     q_frame = jnp.maximum((q_row & 7) + 8, first_frame)
     k_frame = k_col & 15
     allowed = ((q_row >> 3) == (k_col >> 4)) & (k_frame <= q_frame) & (k_frame >= first_frame)
-    for g in range(5):
-        q = queries[64 * g : 64 * g + 64]
-        k = keys[128 * g : 128 * g + 128]
-        v = values[128 * g : 128 * g + 128]
-        scores = lax.dot_general(q, k, (((1,), (1,)), ((), ())), preferred_element_type=F32) * C ** (-0.5)
-        scores = jnp.where(allowed, scores, -1e30)
-        weights = jnp.exp(scores - jnp.max(scores, axis=1, keepdims=True))
-        weights = jnp.where(allowed, weights, 0.0)
-        total = jnp.sum(weights, axis=1, keepdims=True)
-        summed = jnp.dot(weights.astype(BF16), v, preferred_element_type=F32)
-        attended[64 * g : 64 * g + 64] = (summed / total).astype(BF16)
+
+    def attend(groups):
+        scores = [
+            lax.dot_general(
+                queries[64 * g : 64 * g + 64], keys[128 * g : 128 * g + 128], (((1,), (1,)), ((), ())),
+                preferred_element_type=F32,
+            )
+            for g in groups
+        ]
+        weights, totals = [], []
+        for part in scores:
+            part = jnp.where(allowed, part * C ** (-0.5), -1e30)
+            part = jnp.exp(part - jnp.max(part, axis=1, keepdims=True))
+            part = jnp.where(allowed, part, 0.0)
+            totals.append(jnp.sum(part, axis=1, keepdims=True))
+            weights.append(part.astype(BF16))
+        summed = [
+            jnp.dot(part, values[128 * g : 128 * g + 128], preferred_element_type=F32) for part, g in zip(weights, groups)
+        ]
+        for part, total, g in zip(summed, totals, groups):
+            attended[64 * g : 64 * g + 64] = (part / total).astype(BF16)
+
+    line(0, 0)
+    line(128, 8)
+    project(0, 16)
+    block_copy(0).wait_recv()
+    pl.when(first_core)(lambda: ring_forward(0, 1).start())
+    pass_on(block_copy, ring_forward)
+    attend((0, 1))
+    await_passed(block_copy)
+    line(256, 16)
+    line(384, 24)
+    for at, cell in ((512, 32), (544, 34)):
+        parts = rows_of(at, 8)
+        place([cell], parts, 0)
+        place([cell + 1], parts, 1)
+    for i in range(4):
+        place([36 + i], corner_of(RING_AT[i]), 0)
+    project(16, 40)
+    attend((2, 3, 4))
 
     projected = jnp.dot(attended[...], wout[...], preferred_element_type=F32).reshape(CELLS, 8, C)
     top, bottom = tile_row == 0, tile_row == GRID_ROWS - 1
     leftmost, rightmost = tile_col == 0, tile_col == GRID_COLS - 1
     for r in range(4):
-        mixed = (xhi[10 * r : 10 * r + 10] + (projected[10 * r : 10 * r + 10] + bout[...])).astype(BF16).astype(F32)
+        cells = ((36, 16, 37), (32, 0, 34), (33, 8, 35), (38, 24, 39))[r]
+        picks = (slice(cells[0], cells[0] + 1), slice(cells[1], cells[1] + 8), slice(cells[2], cells[2] + 1))
+        mixed = jnp.concatenate([xhi[p] + (projected[p] + bout[...]) for p in picks], axis=0).astype(BF16).astype(F32)
         col = iota((10, 8, C), 0)
         outside = (leftmost & (col == 0)) | (rightmost & (col == 9))
         if r == 0:
@@ -355,13 +396,13 @@
 
     lax.fori_loop(0, 27, wait_first, 0)
 
-    def first_taps(e, carry):
+    def first_taps(e):
         for b in range(3):
             begin, end = ((0, 240), (0, 320), (80, 320))[b]
             t1[b, e, begin:end] = jnp.dot(mixcat[begin:end], w1[3 * b + e], preferred_element_type=F32)
-        return carry
-
-    lax.fori_loop(0, 3, first_taps, 0)
+
+    for e in range(3):
+        first_taps(e)
 
     def t1_row(b, e, r, lanes):
         return t1[b, e, 80 * r : 80 * r + 80, lanes].reshape(10, 8, LANES)
@@ -417,22 +458,22 @@
         rows = by_frame(stats_before[which], stats_own[which], (0, 0, 1, 1, 1, 1, 1, 1), (2, 3, 0, 1, 2, 3, 3, 3))
         rows = jnp.where(starting & (row8 < 2), jnp.broadcast_to(rows[2:3], (8, LANES)), rows)
         pair.append(spread(rows))
-    mean2, scale2 = pair[0], pair[1] * gain2[...]
+    mean2, scale2, bias2h = pair[0], pair[1] * (0.5 * gain2[...]), 0.5 * bias2[...]
     low4 = iota((1, 8, LANES), 1) < 4
-    index9 = iota((9, 8, LANES), 0)
     for R in range(6):
         for k in range(CHUNKS):
             lanes = slice(k * LANES, (k + 1) * LANES)
             both = []
             for parity in range(2):
-                v = (fs[R, parity, :, :, lanes] - mean2[:, lanes]) * scale2[:, lanes] + bias2[:, lanes]
-                v = 0.5 * v * (1.0 + jnp.tanh(0.5 * v))
-                outside = (rightmost & (index9 == 8)) if parity else (leftmost & (index9 == 0))
-                if R == 0:
-                    outside = outside | top
-                if R == 5:
-                    outside = outside | bottom
-                both.append(jnp.where(outside, 0.0, v))
+                v = (fs[R, parity, :, :, lanes] - mean2[:, lanes]) * scale2[:, lanes] + bias2h[:, lanes]
+                v = v + v * jnp.tanh(v)
+                edge = 8 if parity else 0
+                gone = rightmost if parity else leftmost
+                if R in (0, 5):
+                    missing = top if R == 0 else bottom
+                    v = jnp.where(missing, 0.0, v)
+                kept = jnp.where(gone, 0.0, v[edge : edge + 1])
+                both.append(jnp.concatenate([v[0:8], kept] if parity else [kept, v[1:9]], axis=0))
             for a in range(3):
                 joined = []
                 for parity in range(2):
@@ -442,13 +483,13 @@
                 tile = jnp.concatenate(joined, axis=1).reshape(80, LANES).astype(BF16)
                 actcat[80 * R : 80 * R + 80, a * C + k * LANES : a * C + (k + 1) * LANES] = tile
 
-    def second_taps(e, carry):
+    def second_taps(e):
         for b in range(3):
             begin, end = ((0, 400), (80, 400), (80, 480))[b]
             t2[b, e, begin:end] = jnp.dot(actcat[begin:end], w2[3 * b + e], preferred_element_type=F32)
-        return carry
-
-    lax.fori_loop(0, 3, second_taps, 0)
+
+    for e in range(3):
+        second_taps(e)
 
     to, fro = iota((128, 128), 0), iota((128, 128), 1)
     place_f, place_col = to >> 5, to & 31
@@ -470,9 +511,19 @@
             out_ref[f, row] = final[32 * f : 32 * f + 32]
 
     block_copy(0).wait_send()
-    pl.when(tm < 2)(lambda: block_copy(2).wait_send())
-    pl.when(first_core)(lambda: forward(0, 1).wait_send())
-    pl.when(tm >= 2)(lambda: forward(2, 1).wait_send())
+    pl.when(first_core)(lambda: ring_forward(0, 1).wait_send())
+    pl.when(first_core)(lambda: centre_forward(0, 1).wait_send())
+
+    @pl.when(tm < 2)
+    def _():
+        block_copy(2).wait_send()
+        centre_copy(2).wait_send()
+
+    @pl.when(tm >= 2)
+    def _():
+        ring_forward(2, 1).wait_send()
+        centre_forward(2, 1).wait_send()
+
     sums_copy(0, got1, 256).wait_send()
     sums_copy(1, got2, 128).wait_send()
 
@@ -484,7 +535,7 @@
     any_spec = pl.BlockSpec(memory_space=pl.ANY)
     decoded = pl.pallas_call(
         kernel,
-        out_shape=jax.ShapeDtypeStruct((FRAMES, 8, 32, C2), BF16),
+        out_shape=pltpu.VMEM((FRAMES, 8, 32, C2), BF16),
         in_specs=[any_spec] * 12,
         out_specs=pl.BlockSpec(memory_space=pltpu.VMEM),
         scratch_shapes=[
@@ -522,6 +573,9 @@
             pltpu.SemaphoreType.DMA((SHARDS,)),
             pltpu.SemaphoreType.DMA((SHARDS,)),
             pltpu.SemaphoreType.DMA((2,)),
+            pltpu.SemaphoreType.DMA((SHARDS,)),
+            pltpu.SemaphoreType.DMA((SHARDS,)),
+            pltpu.SemaphoreType.DMA((2,)),
             pltpu.SemaphoreType.DMA((2,)),
             pltpu.SemaphoreType.DMA((2,)),
         ],

time: 41.1 us -> 36.2 us (0.88)
  the two profiles are of different devices: /device:TPU:1 before, /device:TPU:25 now
where the time goes in v3:
time: 36.2 us; the launch traced here: 36.1 us
  Pallas kernels  35.3 us (98%)
  local copies, waits for them, and re-layouts  0.8 us (2%)
    pallas_call x1, Pallas kernels, per_device(): pl.pallas_call(kernel, out_shape=pltpu.VMEM((FRAMES, 8, 32, C2), BF16), i...  35.3 us
    unnamed x1, local copies, waits for them, and re-layouts  0.8 us

profile of v3, /device:TPU:25, one launch (start us, length us, event | category | flops | bytes accessed | tf_op | source)
XLA Modules:
  0.0 36.1 jit_solution(3959911165587699235)
XLA Ops:
  0.0 35.3 %shard_map.118 = bf16[4,8,32,256]{3,2,1,0:T(8,128)(2,1)S(1)} custom-call(bf16[4,2,8,512]{3,2,1,0:T(8,128)(2,1)} %bitcast.16, f32[1,512]{1,0:T(1,128)} %bitcast.17, f32[1,512]{1,0:T(1,128)} %bitcast.18, bf16[512,1536]{1,0:T(8,128)(2,1)} %wqkv_hbm.1, bf16[512,512]{1,0:T(8,128)(2,1)} %wout_hbm.1, f32[1,512]{1,0:T(1,128)} %bitcast.19, ...), custom_call_target="tpu_custom_call" | custom-call | tf_op jit(solution)/shard_map/pallas_call | solution.py:536
  35.3 0.8 %copy.15 = bf16[4,1,8,32,256]{4,3,2,1,0:T(8,128)(2,1)} copy(bf16[4,1,8,32,256]{4,3,2,1,0:T(8,128)(2,1)S(1)} %bitcast.13) | data formatting | bytes 1048576

commit v4 on v3

--- a/solution.py
+++ b/solution.py
@@ -61,9 +61,16 @@
 
 
 def group_stats(block, count):
+    return row_stats(block_total(block), count)
+
+
+def block_total(block):
     total = jnp.sum(block.reshape(8, 8, LANES), axis=0)
     total = total + sub_roll(total, 2)
-    total = total + sub_roll(total, 4)
+    return total + sub_roll(total, 4)
+
+
+def row_stats(total, count):
     mean = total[0:1] * (1.0 / count)
     square = total[1:2] * (1.0 / count)
     scale = lax.rsqrt(square - mean * mean + EPS)
@@ -96,8 +103,8 @@
     hid_hbm, gain1_hbm, bias1_hbm, wqkv_hbm, wout_hbm, bout_hbm, w1_hbm, b1_hbm, gain2_hbm, bias2_hbm, w2_hbm, b2_hbm,
     out_ref,
     hid, gain1, bias1, wqkv, wout, bout, w1, b1, gain2, bias2, w2, b2,
-    side, hbuf, sums, got1, got2, xhi, normed, queries, keys, values, attended, mixcat, t1, fs, actcat, t2,
-    small_sem, w1_sem, w2_sem, hid_send, hid_recv, pass_send, cen_send, cen_recv, cpass_send, sum_send, sum_recv,
+    side, hbuf, sums, got1, got2, pair_out, pair_in, xhi, normed, queries, keys, wmix, attended, mixcat, t1, fs, actcat, t2,
+    small_sem, w1_sem, w2_sem, hid_send, hid_recv, pass_send, cen_send, cen_recv, cpass_send, sum_send, sum_recv, pair_sem,
 ):
     tm = lax.axis_index("tm")
     sp = lax.axis_index("space")
@@ -116,8 +123,13 @@
         copy.start()
 
     barrier = pltpu.get_barrier_semaphore()
+    def greet(shard, tile):
+        pl.semaphore_signal(barrier, inc=1, device_id=(shard, tile), device_id_type=MESH)
+
     for kt, ks in PEERS:
-        pl.semaphore_signal(barrier, inc=1, device_id=(tm ^ kt, sp ^ ks), device_id_type=MESH)
+        if kt != 3:
+            greet((tm + 3) & 3 if kt == 1 else tm ^ kt, sp ^ ks)
+    pl.when((tm & 1) == 0)(lambda: greet(tm + 1, sp))
 
     def tap_copies(i):
         a, be = i // 9, lax.rem(i, 9)
@@ -172,7 +184,9 @@
     sums[0] = packed
     got1[0:2] = packed
 
-    pl.semaphore_wait(barrier, SHARDS * TILES - 1)
+    wmix[...] = jnp.dot(wqkv[:, 2 * C :], wout[...], preferred_element_type=F32).astype(BF16)
+
+    pl.semaphore_wait(barrier, 3 * TILES - 1 + (tm & 1))
 
     def send_sums(which, target, slot, buf):
         pltpu.make_async_remote_copy(
@@ -181,7 +195,8 @@
         ).start()
 
     for kt, ks in PEERS:
-        send_sums(0, (tm ^ kt, sp ^ ks), kt * TILES + ks, got1)
+        if kt in (0, 2):
+            send_sums(0, (tm ^ kt, sp ^ ks), (kt // 2) * TILES + ks, got1)
 
     def piece(dr, dc):
         if dc == 0:
@@ -255,14 +270,26 @@
     pl.when(first_core)(lambda: centre_forward(0, 1).start())
     pass_on(centre_copy, centre_forward)
     await_passed(centre_copy)
-    sums_copy(0, got1, 256).wait_recv()
+    sums_copy(0, got1, 128).wait_recv()
 
     starting = tm == 0
     row8 = iota((8, LANES), 0)
-    stats = []
-    for dt in range(SHARDS):
-        kt = tm ^ ((tm - dt) & 3)
-        stats.append(group_stats(got1[pl.ds(pl.multiple_of(kt * 64, 64), 64)], TILES * 16 * 16))
+    mine_two = jnp.where(row8 < 2, block_total(got1[0:64]), block_total(got1[64:128]))
+    pair_out[...] = mine_two
+    pair_copy = pltpu.make_async_remote_copy(
+        src_ref=pair_out, dst_ref=pair_in, send_sem=pair_sem.at[0], recv_sem=pair_sem.at[1],
+        device_id=(tm ^ 1, sp), device_id_type=MESH,
+    )
+    pair_copy.start()
+    pair_copy.wait()
+    other_two = pair_in[...]
+    near, far = other_two[0:2], other_two[2:4]
+    stats = [
+        row_stats(total, TILES * 16 * 16)
+        for total in (
+            mine_two[0:2], jnp.where(first_core, far, near), mine_two[2:4], jnp.where(first_core, near, far),
+        )
+    ]
     span = (0, 0, 0, 0, 1, 1, 1, 1)
     steps = (0, 1, 2, 3, 0, 1, 2, 3)
     normers = []
@@ -324,7 +351,6 @@
         queries[asking] = jnp.dot(queries[asking], wqkv[:, 0:C], preferred_element_type=F32).astype(BF16)
         part = normed[begin:end].reshape((end - begin) * 16, C)
         keys[rows] = jnp.dot(part, wqkv[:, C : 2 * C], preferred_element_type=F32).astype(BF16)
-        values[rows] = jnp.dot(part, wqkv[:, 2 * C :], preferred_element_type=F32).astype(BF16)
 
     q_row, k_col = iota((64, 128), 0), iota((64, 128), 1)
     first_frame = 12 - 4 * tm
@@ -348,7 +374,8 @@
             totals.append(jnp.sum(part, axis=1, keepdims=True))
             weights.append(part.astype(BF16))
         summed = [
-            jnp.dot(part, values[128 * g : 128 * g + 128], preferred_element_type=F32) for part, g in zip(weights, groups)
+            jnp.dot(part, normed[8 * g : 8 * g + 8].reshape(128, C), preferred_element_type=F32)
+            for part, g in zip(weights, groups)
         ]
         for part, total, g in zip(summed, totals, groups):
             attended[64 * g : 64 * g + 64] = (part / total).astype(BF16)
@@ -372,7 +399,7 @@
     project(16, 40)
     attend((2, 3, 4))
 
-    projected = jnp.dot(attended[...], wout[...], preferred_element_type=F32).reshape(CELLS, 8, C)
+    projected = jnp.dot(attended[...], wmix[...], preferred_element_type=F32).reshape(CELLS, 8, C)
     top, bottom = tile_row == 0, tile_row == GRID_ROWS - 1
     leftmost, rightmost = tile_col == 0, tile_col == GRID_COLS - 1
     for r in range(4):
@@ -524,7 +551,7 @@
         ring_forward(2, 1).wait_send()
         centre_forward(2, 1).wait_send()
 
-    sums_copy(0, got1, 256).wait_send()
+    sums_copy(0, got1, 128).wait_send()
     sums_copy(1, got2, 128).wait_send()
 
 
@@ -554,13 +581,15 @@
             pltpu.VMEM((128, LANES), BF16),
             pltpu.VMEM((4, BLOCK_ROWS, LANES), BF16),
             pltpu.VMEM((2, 2, LANES), F32),
-            pltpu.VMEM((256, LANES), F32),
             pltpu.VMEM((128, LANES), F32),
+            pltpu.VMEM((128, LANES), F32),
+            pltpu.VMEM((8, LANES), F32),
+            pltpu.VMEM((8, LANES), F32),
             pltpu.VMEM((CELLS, 8, C), F32),
             pltpu.VMEM((CELLS, 16, C), BF16),
             pltpu.VMEM((CELLS * 8, C), BF16),
             pltpu.VMEM((CELLS * 16, C), BF16),
-            pltpu.VMEM((CELLS * 16, C), BF16),
+            pltpu.VMEM((C, C), BF16),
             pltpu.VMEM((CELLS * 8, C), BF16),
             pltpu.VMEM((CELLS * 8, 3 * C), BF16),
             pltpu.VMEM((3, 3, CELLS * 8, C), F32),
@@ -575,6 +604,7 @@
             pltpu.SemaphoreType.DMA((2,)),
             pltpu.SemaphoreType.DMA((SHARDS,)),
             pltpu.SemaphoreType.DMA((SHARDS,)),
+            pltpu.SemaphoreType.DMA((2,)),
             pltpu.SemaphoreType.DMA((2,)),
             pltpu.SemaphoreType.DMA((2,)),
             pltpu.SemaphoreType.DMA((2,)),

time: 36.2 us -> 36 us (level)
  the two profiles are of different devices: /device:TPU:25 before, /device:TPU:1 now
where the time goes in v4:
time: 36 us; the launch traced here: 35.9 us
  Pallas kernels  35.1 us (98%)
  local copies, waits for them, and re-layouts  0.8 us (2%)
    pallas_call x1, Pallas kernels, per_device(): pl.pallas_call(kernel, out_shape=pltpu.VMEM((FRAMES, 8, 32, C2), BF16), i...  35.1 us
    unnamed x1, local copies, waits for them, and re-layouts  0.8 us

profile of v4, /device:TPU:1, one launch (start us, length us, event | category | flops | bytes accessed | tf_op | source)
XLA Modules:
  0.0 35.9 jit_solution(12616928029683554741)
XLA Ops:
  0.0 35.1 %shard_map.118 = bf16[4,8,32,256]{3,2,1,0:T(8,128)(2,1)S(1)} custom-call(bf16[4,2,8,512]{3,2,1,0:T(8,128)(2,1)} %bitcast.16, f32[1,512]{1,0:T(1,128)} %bitcast.17, f32[1,512]{1,0:T(1,128)} %bitcast.18, bf16[512,1536]{1,0:T(8,128)(2,1)} %wqkv_hbm.1, bf16[512,512]{1,0:T(8,128)(2,1)} %wout_hbm.1, f32[1,512]{1,0:T(1,128)} %bitcast.19, ...), custom_call_target="tpu_custom_call" | custom-call | tf_op jit(solution)/shard_map/pallas_call | solution.py:563
  35.1 0.8 %copy.15 = bf16[4,1,8,32,256]{4,3,2,1,0:T(8,128)(2,1)} copy(bf16[4,1,8,32,256]{4,3,2,1,0:T(8,128)(2,1)S(1)} %bitcast.13) | data formatting | bytes 1048576

commit v5 on v3

--- a/solution.py
+++ b/solution.py
@@ -396,19 +396,11 @@
 
     lax.fori_loop(0, 27, wait_first, 0)
 
-    def first_taps(e):
-        for b in range(3):
-            begin, end = ((0, 240), (0, 320), (80, 320))[b]
-            t1[b, e, begin:end] = jnp.dot(mixcat[begin:end], w1[3 * b + e], preferred_element_type=F32)
-
-    for e in range(3):
-        first_taps(e)
-
     def t1_row(b, e, r, lanes):
         return t1[b, e, 80 * r : 80 * r + 80, lanes].reshape(10, 8, LANES)
 
     sum_first, sum_second = [], []
-    for k in range(CHUNKS):
+    def gather_chunk(k):
         lanes = slice(k * LANES, (k + 1) * LANES)
         acc, acc2 = jnp.zeros((8, LANES), F32), jnp.zeros((8, LANES), F32)
         for R in range(6):
@@ -432,6 +424,18 @@
                 acc2 = acc2 + jnp.sum(inner_e * inner_e, axis=0) + jnp.sum(inner_o * inner_o, axis=0)
         sum_first.append(acc)
         sum_second.append(acc2)
+
+    for n in range(2):
+        cols = slice(256 * n, 256 * n + 256)
+        for e in range(3):
+            for b in range(3):
+                begin, end = ((0, 240), (0, 320), (80, 320))[b]
+                t1[b, e, begin:end, cols] = jnp.dot(
+                    mixcat[begin:end], w1[3 * b + e, :, cols], preferred_element_type=F32
+                )
+        for k in range(2 * n, 2 * n + 2):
+            gather_chunk(k)
+
     packed = jnp.concatenate(
         [pack_sums(jnp.concatenate(sum_first, axis=1), 2), pack_sums(jnp.concatenate(sum_second, axis=1), 2)], axis=0
     )

time: 36.2 us -> 36.1 us (level)
  no operation moved by 1% of the time
where the time goes in v5:
time: 36.1 us; the launch traced here: 36 us
  Pallas kernels  35.2 us (98%)
  local copies, waits for them, and re-layouts  0.8 us (2%)
    pallas_call x1, Pallas kernels, per_device(): pl.pallas_call(kernel, out_shape=pltpu.VMEM((FRAMES, 8, 32, C2), BF16), i...  35.2 us
    unnamed x1, local copies, waits for them, and re-layouts  0.8 us

profile of v5, /device:TPU:25, one launch (start us, length us, event | category | flops | bytes accessed | tf_op | source)
XLA Modules:
  0.0 36.0 jit_solution(13755724194628067057)
XLA Ops:
  0.0 35.2 %shard_map.118 = bf16[4,8,32,256]{3,2,1,0:T(8,128)(2,1)S(1)} custom-call(bf16[4,2,8,512]{3,2,1,0:T(8,128)(2,1)} %bitcast.16, f32[1,512]{1,0:T(1,128)} %bitcast.17, f32[1,512]{1,0:T(1,128)} %bitcast.18, bf16[512,1536]{1,0:T(8,128)(2,1)} %wqkv_hbm.1, bf16[512,512]{1,0:T(8,128)(2,1)} %wout_hbm.1, f32[1,512]{1,0:T(1,128)} %bitcast.19, ...), custom_call_target="tpu_custom_call" | custom-call | tf_op jit(solution)/shard_map/pallas_call | solution.py:540
  35.2 0.8 %copy.15 = bf16[4,1,8,32,256]{4,3,2,1,0:T(8,128)(2,1)} copy(bf16[4,1,8,32,256]{4,3,2,1,0:T(8,128)(2,1)S(1)} %bitcast.13) | data formatting | bytes 1048576
